TPU v7x, 512 devices: a whole 4x4x16 slice. The times are simulated.
512 devices in a mesh: row: 16 (over x, z_lo), col: 32 (over z_hi, y, core).
Axes of the slice: x: 4, y: 4, z: 16 (z_hi: 4, z_lo: 4; z = z_hi * 4 + z_lo), core: 2. Of those that a mesh axis runs over, the one named last changes fastest.
Arguments:
- left_vals: bfloat16 [12288, 4096], P('row', 'col'), may hold values from -6 to 6
- left_scale: float32 [96, 32], P('row', 'col'), may hold values from 0.02 to 0.2
- left_keep: int32 [96, 32], P('row', 'col'), may hold values 0 or 1
- right_vals: bfloat16 [4096, 24576], P('row', 'col'), may hold values from -6 to 6
- right_scale: float32 [32, 192], P('row', 'col'), may hold values from 0.02 to 0.35, as said below
- right_keep: int32 [32, 192], P('row', 'col'), may hold values 0 or 1
- result_keep: int32 [96, 192], P('row', 'col'), may hold values 0 or 1
Outputs:
- flow: float32 [12288, 24576], P('row', 'col')
Inputs may be any that keep to these rules, and one draw needn't show every extreme that they name: `right_scale`: each tile's scale, positive.
All inputs are finite; a program needn't handle non-finite values. No bound on the sum of `left_keep` or of `right_keep` or of `result_keep` on one device may be relied on, other than what follows from the above.
Results may differ from a plain program's by a relative error of at most 0.0047.
Values may be sent and summed in bfloat16 or wider, within the bound.
No kernel may reach another device: no remote copies, remote signals or barrier semaphores. Data moves between devices by JAX's collectives and lax.ppermute only.
A program may use at most 64 MiB of HBM per device.

v0:
```python
import jax
import jax.numpy as jnp
from jax import lax
from jax.sharding import PartitionSpec as P


def tiled(values, scales, keep):
    rows, cols = scales.shape
    size = values.shape[0] // rows
    factor = scales * keep.astype(jnp.float32)
    shaped = values.astype(jnp.float32).reshape(rows, size, cols, size) * factor[:, None, :, None]
    return shaped.reshape(values.shape).astype(jnp.bfloat16)


def per_device(left_vals, left_scale, left_keep, right_vals, right_scale, right_keep, result_keep):
    left_tiles = tiled(left_vals, left_scale, left_keep)
    right_tiles = tiled(right_vals, right_scale, right_keep)
    right_full = lax.all_gather(right_tiles, "row", axis=0, tiled=True)
    product = jnp.dot(
        lax.all_gather(left_tiles, "col", axis=1, tiled=True),
        right_full,
        preferred_element_type=jnp.float32,
    )
    size = left_vals.shape[0] // left_scale.shape[0]
    keep_wide = jnp.repeat(jnp.repeat(result_keep.astype(jnp.float32), size, axis=0), size, axis=1)
    pruned = product * product * keep_wide
    partial_totals = jnp.sum(pruned, axis=1, keepdims=True)
    totals = lax.psum(partial_totals, "col")
    width = right_vals.shape[1] * lax.axis_size("col")
    return width * pruned / (totals + 1e-06)


def solution(mesh):
    return jax.shard_map(
        per_device,
        mesh=mesh,
        in_specs=(
            P("row", "col"),
            P("row", "col"),
            P("row", "col"),
            P("row", "col"),
            P("row", "col"),
            P("row", "col"),
            P("row", "col"),
        ),
        out_specs=P("row", "col"),
        check_vma=False,
    )
```

profile of v0, /device:TPU:1, one launch (start us, length us, event | category | flops | bytes accessed | tf_op | source)
XLA Modules:
  0.0 401.5 jit_solution(6759275633172935953)
XLA Ops:
  6.5 0.0 copy-start.3
  6.5 0.0 copy-start.2
  6.5 0.0 copy-start
  6.5 0.0 copy-start.1
  6.5 0.0 all-gather.5.cloned.1.call-start
  6.6 0.8 convert_multiply_fusion
  7.4 0.1 copy.11
  7.5 1.2 copy.10
  8.6 0.3 mul.53
  8.9 0.8 fusion.1
  9.8 0.0 all-gather.5.cloned.1.call-update
  9.8 0.0 all-gather.3.cloned.1.call-start
  9.8 0.0 copy-done.3
  9.8 0.0 copy-done.2
  9.9 0.1 broadcast_bitcast_fusion.1
  9.9 0.0 copy-done
  9.9 0.9 multiply_convert_fusion
  10.8 0.0 all-gather.3.cloned.1.call-update
  10.8 0.0 copy-done.1
  10.8 0.1 copy.12
  10.9 0.1 broadcast_bitcast_fusion
  11.0 153.8 %all-gather.5.cloned.1.call-done = bf16[4096,768]{0,1:T(8,128)(2,1)} async-done(((bf16[256,768]{0,1:T(8,128)(2,1)}), bf16[4096,768]{0,1:T(8,128)(2,1)}) %all-gather.5.cloned.1.call-update) | async-done | bytes 6291472 | tf_op jit(solution)/shard_map/all_gather | solution.py:18
  164.8 130.9 %all-gather.3.cloned.1.call-done = bf16[768,4096]{1,0:T(8,128)(2,1)} async-done(((bf16[768,128]{1,0:T(8,128)(2,1)}), bf16[768,4096]{1,0:T(8,128)(2,1)}) %all-gather.3.cloned.1.call-update) | async-done | bytes 6291472 | tf_op jit(solution)/shard_map/all_gather | solution.py:20
  295.8 11.1 %fusion = (f32[768]{0:T(1024)S(1)}, f32[768,768]{0,1:T(8,128)}) fusion(f32[768,6]{0,1:T(8,128)S(1)} %bitcast.28, bf16[768,4096]{1,0:T(8,128)(2,1)} %all-gather.3.cloned.1.call-done, bf16[4096,768]{0,1:T(8,128)(2,1)} %all-gather.5.cloned.1.call-done), kind=kOutput, calls=%fused_computation.2 | convolution fusion | flops 4833606656 | bytes 14963712 | tf_op jit(solution)/shard_map/dot_general | solution.py:19
  306.9 83.8 %psum.7 = f32[768,1]{0,1:T(1,128)S(1)} all-reduce(f32[768,1]{0,1:T(1,128)S(1)} %broadcast_in_dim.13), channel_id=1, replica_groups=mesh['row'=16,'col'=32] {'col'}, use_global_device_ids=true, to_apply=%region_1.0 | all-reduce | flops 768 | bytes 6144 | tf_op jit(solution)/shard_map/psum | solution.py:28
  390.7 2.0 multiply_divide_fusion
  392.7 2.0 copy.13
  (5 shorter events, 0.0 us)
Async XLA Ops:
  6.5 3.3 copy-start.3
  6.5 3.3 copy-start.2
  6.5 3.4 copy-start
  6.5 4.3 %copy-start.1 = (s32[6,6]{1,0:T(8,128)S(1)}, s32[6,6]{1,0:T(8,128)}, u32[]{:S(2)}) copy-start(s32[6,6]{1,0:T(8,128)} %param.13) | copy-start | bytes 436
  6.5 158.3 %all-gather.5.cloned.1.call-start = ((), (), s32[]{:S(2)}) async-start(), calls=%async_computation.1 | async-start | bytes 6684672 | tf_op jit(solution)/shard_map/all_gather | solution.py:18
  9.8 286.0 %all-gather.3.cloned.1.call-start = ((), (), s32[]{:S(2)}) async-start(), calls=%async_computation | async-start | bytes 6488064 | tf_op jit(solution)/shard_map/all_gather | solution.py:20
Sparse Core Ops, SparseCore 0:
  9.9 154.8 all-gather.4
  167.9 127.8 all-gather.2
where the time goes:
time: 404 us; the launch traced here: 402 us
  waiting for transfers between devices  285 us (71%)
  blocking collectives  83.8 us (21%)
  between operations  13.5 us (3%)
  matrix products  11.1 us (3%)
  other arithmetic  4.51 us (1%)
    all_gather x1, waiting for transfers between devices, per_device(): right_full = lax.all_gather(right_tiles, 'row', axis=0, tiled=True)  154 us
    all_gather x1, waiting for transfers between devices, per_device(): lax.all_gather(left_tiles, 'col', axis=1, tiled=True)  131 us
    psum x1, blocking collectives, per_device(): totals = lax.psum(partial_totals, 'col')  83.8 us
    dot_general x1, matrix products, per_device(): jnp.dot(lax.all_gather(left_tiles, 'col', axis=1, tiled=True), right_full...  11.1 us
  transfers between devices with their start and end apart: 2, of which 2 were waited for; matrix products, arithmetic and copies ran while one was open for 0% of the time, Pallas kernels for 0%

commit v1 on v0

v1 whole, which is shorter than its diff:
```python
import jax
import jax.numpy as jnp
from jax import lax
from jax.experimental import pallas as pl
from jax.experimental.pallas import tpu as pltpu
from jax.sharding import Mesh, PartitionSpec as P

AXES = ("x", "zl", "zh", "y", "core")
SIDE = 4
TILE = 128


def tiled(values, scales, keep):
    rows, cols = scales.shape
    size = values.shape[0] // rows
    factor = scales * keep.astype(jnp.float32)
    shaped = values.astype(jnp.float32).reshape(rows, size, cols, size) * factor[:, None, :, None]
    return shaped.reshape(values.shape).astype(jnp.bfloat16)


def step(value, axis):
    pairs = []
    for i in range(SIDE):
        pairs.append((2 * i, 2 * ((i + 1) % SIDE)))
        pairs.append((2 * i + 1, 2 * ((i - 1) % SIDE) + 1))
    return lax.ppermute(value, (axis, "core"), pairs)


def ring(value, axis):
    blocks = [value]
    for _ in range(SIDE - 1):
        blocks.append(step(blocks[-1], axis))
    return blocks


def multiply(place_ref, keep_ref, own_ref, other_ref, *refs):
    count = SIDE * SIDE
    right_refs = refs[:count]
    pruned_ref, total_ref, left, right, left_sem, right_sem = refs[count:]
    depth = right_refs[0].shape[0]
    half = own_ref.shape[2]
    copies = []
    for i in range(count):
        at = pl.multiple_of(place_ref[i] * half, half)
        copies.append(pltpu.make_async_copy(own_ref.at[i], left.at[:, pl.ds(at, half)], left_sem))
        at = pl.multiple_of(place_ref[count + i] * half, half)
        copies.append(pltpu.make_async_copy(other_ref.at[i], left.at[:, pl.ds(at, half)], left_sem))
        at = pl.multiple_of(place_ref[2 * count + i] * depth, depth)
        copies.append(pltpu.make_async_copy(right_refs[i], right.at[pl.ds(at, depth), :], right_sem))
    for copy in copies:
        copy.start()
    for copy in copies:
        copy.wait()
    rows = 2 * TILE
    for m in range(left.shape[0] // rows):
        product = jnp.dot(left[m * rows:(m + 1) * rows, :], right[...], preferred_element_type=jnp.float32)
        for r in range(rows // TILE):
            total = jnp.zeros((TILE, TILE), jnp.float32)
            at = m * rows + r * TILE
            for n in range(right.shape[1] // TILE):
                block = product[r * TILE:(r + 1) * TILE, n * TILE:(n + 1) * TILE]
                block = block * block * keep_ref[at // TILE, n].astype(jnp.float32)
                pruned_ref[at:at + TILE, n * TILE:(n + 1) * TILE] = block
                total = total + block
            total_ref[at:at + TILE, :] = jnp.sum(total, axis=1, keepdims=True)


def per_device(left_vals, left_scale, left_keep, right_vals, right_scale, right_keep, result_keep):
    x, zl, zh, y, core = (lax.axis_index(a) for a in AXES)
    way = 1 - 2 * core
    right_tiles = tiled(right_vals, right_scale, right_keep)
    left_tiles = tiled(left_vals, left_scale, left_keep)

    right_blocks, right_place = [], []
    for k, lane in enumerate(ring(right_tiles, "zl")):
        for s, block in enumerate(ring(lane, "x")):
            right_blocks.append(block)
            right_place.append((x - s * way) % SIDE * SIDE + (zl - k * way) % SIDE)
    left_blocks, own_place, other_place = [], [], []
    for k, lane in enumerate(ring(left_tiles, "zh")):
        for s, block in enumerate(ring(lane, "y")):
            left_blocks.append(block)
            own_place.append(((zh - k * way) % SIDE * SIDE + (y - s * way) % SIDE) * 2 + core)
            other_place.append(((zh + k * way) % SIDE * SIDE + (y + s * way) % SIDE) * 2 + 1 - core)
    own = jnp.stack(left_blocks)
    other = lax.ppermute(own, "core", [(0, 1), (1, 0)])
    place = jnp.stack(own_place + other_place + right_place).astype(jnp.int32)

    rows, cols = left_vals.shape[0], right_vals.shape[1]
    depth = right_vals.shape[0] * SIDE * SIDE
    smem = pl.BlockSpec(memory_space=pltpu.SMEM)
    vmem = pl.BlockSpec(memory_space=pltpu.VMEM)
    hbm = pl.BlockSpec(memory_space=pl.ANY)
    pruned, partial_totals = pl.pallas_call(
        multiply,
        out_shape=(
            jax.ShapeDtypeStruct((rows, cols), jnp.float32),
            jax.ShapeDtypeStruct((rows, 1), jnp.float32),
        ),
        in_specs=[smem, smem, hbm, hbm] + [hbm] * len(right_blocks),
        out_specs=(vmem, vmem),
        scratch_shapes=[
            pltpu.VMEM((rows, depth), jnp.bfloat16),
            pltpu.VMEM((depth, cols), jnp.bfloat16),
            pltpu.SemaphoreType.DMA,
            pltpu.SemaphoreType.DMA,
        ],
        compiler_params=pltpu.CompilerParams(vmem_limit_bytes=32 * 1024 * 1024),
    )(place, result_keep, own, other, *right_blocks)
    totals = partial_totals
    for axis in ("core", "y", "zh"):
        totals = lax.psum(totals, axis)
    width = cols * lax.axis_size("zh") * lax.axis_size("y") * lax.axis_size("core")
    return width * pruned / (totals + 1e-06)


def solution(mesh):
    fine = Mesh(mesh.devices.reshape(SIDE, SIDE, SIDE, SIDE, 2), AXES)
    spec = P(("x", "zl"), ("zh", "y", "core"))
    return jax.shard_map(
        per_device,
        mesh=fine,
        in_specs=(spec,) * 7,
        out_specs=spec,
        check_vma=False,
    )
```

time: 404 us -> 264 us (0.65)
  the two profiles are of different devices: /device:TPU:1 before, /device:TPU:2 now
where the time goes in v1:
time: 264 us; the launch traced here: 263 us
  starting transfers between devices  113 us (43%)
  blocking collectives  64.9 us (25%)
  waiting for transfers between devices  50.5 us (19%)
  local copies, waits for them, and re-layouts  18.6 us (7%)
  Pallas kernels  9.76 us (4%)
  other arithmetic  5.01 us (2%)
    ppermute x30, starting transfers between devices, step(): return lax.ppermute(value, (axis, 'core'), pairs)  111 us
    psum x3, blocking collectives, per_device(): totals = lax.psum(totals, axis)  64.9 us
    ppermute x30, waiting for transfers between devices, step(): return lax.ppermute(value, (axis, 'core'), pairs)  50.4 us
    unnamed x55, local copies, waits for them, and re-layouts  15.8 us
    pallas_call x1, Pallas kernels, per_device(): pl.pallas_call(multiply, out_shape=(jax.ShapeDtypeStruct((rows, cols), jn...  9.76 us
  transfers between devices with their start and end apart: 31, of which 11 were waited for; matrix products, arithmetic and copies ran while one was open for 2% of the time, Pallas kernels for 0%

profile of v1, /device:TPU:2, one launch (start us, length us, event | category | flops | bytes accessed | tf_op | source)
XLA Modules:
  0.0 262.6 jit_solution(826742589916171104)
XLA Ops:
  0.8 1.1 bitcast_dynamic-update-slice_fusion.15
  1.9 9.1 %collective-permute-start.3 = (bf16[768,128]{1,0:T(8,128)(2,1)S(1)}, bf16[768,128]{1,0:T(8,128)(2,1)S(1)}, u32[]{:S(2)}, u32[]{:S(2)}) collective-permute-start(bf16[768,128]{1,0:T(8,128)(2,1)S(1)} %get-tuple-element.10), channel_id=1, source_target_pairs={{0,8},{1,25},{8,16},{9,1},{16,24},{17,9},{24,0},{25,17},{2,10},{3,... | collective-permute-start | bytes 589832 | tf_op jit(solution)/shard_map/ppermute | solution.py:26
  11.0 3.5 %collective-permute-start = (bf16[768,128]{1,0:T(8,128)(2,1)S(1)}, bf16[768,128]{1,0:T(8,128)(2,1)S(1)}, u32[]{:S(2)}, u32[]{:S(2)}) collective-permute-start(bf16[768,128]{1,0:T(8,128)(2,1)S(1)} %get-tuple-element.10), channel_id=1, source_target_pairs={{0,2},{1,7},{2,4},{3,1},{4,6},{5,3},{6,0},{7,5},{8,10},{9,15},{10,... | collective-permute-start | bytes 589832 | tf_op jit(solution)/shard_map/ppermute | solution.py:26
  14.5 4.1 %collective-permute-done.3 = bf16[768,128]{1,0:T(8,128)(2,1)S(1)} collective-permute-done((bf16[768,128]{1,0:T(8,128)(2,1)S(1)}, bf16[768,128]{1,0:T(8,128)(2,1)S(1)}, u32[]{:S(2)}, u32[]{:S(2)}) %collective-permute-start.3) | collective-permute-done | bytes 196640 | tf_op jit(solution)/shard_map/ppermute | solution.py:26
  18.6 10.8 %collective-permute-start.7 = (bf16[768,128]{1,0:T(8,128)(2,1)S(1)}, bf16[768,128]{1,0:T(8,128)(2,1)S(1)}, u32[]{:S(2)}, u32[]{:S(2)}) collective-permute-start(bf16[768,128]{1,0:T(8,128)(2,1)S(1)} %collective-permute-done.3), channel_id=1, source_target_pairs={{0,8},{1,25},{8,16},{9,1},{16,24},{17,9},{24,0},{25,17},{2,10},{3,... | collective-permute-start | bytes 589832 | tf_op jit(solution)/shard_map/ppermute | solution.py:26
  29.3 3.5 %collective-permute-start.4 = (bf16[768,128]{1,0:T(8,128)(2,1)S(1)}, bf16[768,128]{1,0:T(8,128)(2,1)S(1)}, u32[]{:S(2)}, u32[]{:S(2)}) collective-permute-start(bf16[768,128]{1,0:T(8,128)(2,1)S(1)} %collective-permute-done.3), channel_id=1, source_target_pairs={{0,2},{1,7},{2,4},{3,1},{4,6},{5,3},{6,0},{7,5},{8,10},{9,15},{10,... | collective-permute-start | bytes 589832 | tf_op jit(solution)/shard_map/ppermute | solution.py:26
  32.8 3.5 %collective-permute-start.1 = (bf16[768,128]{1,0:T(8,128)(2,1)S(1)}, bf16[768,128]{1,0:T(8,128)(2,1)S(1)}, u32[]{:S(2)}, u32[]{:S(2)}) collective-permute-start(bf16[768,128]{1,0:T(8,128)(2,1)S(1)} %collective-permute-done), channel_id=1, source_target_pairs={{0,2},{1,7},{2,4},{3,1},{4,6},{5,3},{6,0},{7,5},{8,10},{9,15},{10,... | collective-permute-start | bytes 589832 | tf_op jit(solution)/shard_map/ppermute | solution.py:26
  36.4 8.3 %collective-permute-start.11 = (bf16[768,128]{1,0:T(8,128)(2,1)S(1)}, bf16[768,128]{1,0:T(8,128)(2,1)S(1)}, u32[]{:S(2)}, u32[]{:S(2)}) collective-permute-start(bf16[768,128]{1,0:T(8,128)(2,1)S(1)} %collective-permute-done.7), channel_id=1, source_target_pairs={{0,8},{1,25},{8,16},{9,1},{16,24},{17,9},{24,0},{25,17},{2,10},{3,... | collective-permute-start | bytes 589832 | tf_op jit(solution)/shard_map/ppermute | solution.py:26
  44.7 3.2 %collective-permute-start.8 = (bf16[768,128]{1,0:T(8,128)(2,1)S(1)}, bf16[768,128]{1,0:T(8,128)(2,1)S(1)}, u32[]{:S(2)}, u32[]{:S(2)}) collective-permute-start(bf16[768,128]{1,0:T(8,128)(2,1)S(1)} %collective-permute-done.7), channel_id=1, source_target_pairs={{0,2},{1,7},{2,4},{3,1},{4,6},{5,3},{6,0},{7,5},{8,10},{9,15},{10,... | collective-permute-start | bytes 589832 | tf_op jit(solution)/shard_map/ppermute | solution.py:26
  47.9 2.6 collective-permute-start.2
  50.5 3.2 %collective-permute-start.5 = (bf16[768,128]{1,0:T(8,128)(2,1)S(1)}, bf16[768,128]{1,0:T(8,128)(2,1)S(1)}, u32[]{:S(2)}, u32[]{:S(2)}) collective-permute-start(bf16[768,128]{1,0:T(8,128)(2,1)S(1)} %collective-permute-done.4), channel_id=1, source_target_pairs={{0,2},{1,7},{2,4},{3,1},{4,6},{5,3},{6,0},{7,5},{8,10},{9,15},{10,... | collective-permute-start | bytes 589832 | tf_op jit(solution)/shard_map/ppermute | solution.py:26
  53.8 3.0 %collective-permute-done.11 = bf16[768,128]{1,0:T(8,128)(2,1)S(1)} collective-permute-done((bf16[768,128]{1,0:T(8,128)(2,1)S(1)}, bf16[768,128]{1,0:T(8,128)(2,1)S(1)}, u32[]{:S(2)}, u32[]{:S(2)}) %collective-permute-start.11) | collective-permute-done | bytes 196640 | tf_op jit(solution)/shard_map/ppermute | solution.py:26
  56.8 3.5 %collective-permute-start.12 = (bf16[768,128]{1,0:T(8,128)(2,1)S(1)}, bf16[768,128]{1,0:T(8,128)(2,1)S(1)}, u32[]{:S(2)}, u32[]{:S(2)}) collective-permute-start(bf16[768,128]{1,0:T(8,128)(2,1)S(1)} %collective-permute-done.11), channel_id=1, source_target_pairs={{0,2},{1,7},{2,4},{3,1},{4,6},{5,3},{6,0},{7,5},{8,10},{9,15},{10,... | collective-permute-start | bytes 589832 | tf_op jit(solution)/shard_map/ppermute | solution.py:26
  60.4 3.5 %collective-permute-start.9 = (bf16[768,128]{1,0:T(8,128)(2,1)S(1)}, bf16[768,128]{1,0:T(8,128)(2,1)S(1)}, u32[]{:S(2)}, u32[]{:S(2)}) collective-permute-start(bf16[768,128]{1,0:T(8,128)(2,1)S(1)} %collective-permute-done.8), channel_id=1, source_target_pairs={{0,2},{1,7},{2,4},{3,1},{4,6},{5,3},{6,0},{7,5},{8,10},{9,15},{10,... | collective-permute-start | bytes 589832 | tf_op jit(solution)/shard_map/ppermute | solution.py:26
  63.9 3.2 %collective-permute-start.6 = (bf16[768,128]{1,0:T(8,128)(2,1)S(1)}, bf16[768,128]{1,0:T(8,128)(2,1)S(1)}, u32[]{:S(2)}, u32[]{:S(2)}) collective-permute-start(bf16[768,128]{1,0:T(8,128)(2,1)S(1)} %collective-permute-done.5), channel_id=1, source_target_pairs={{0,2},{1,7},{2,4},{3,1},{4,6},{5,3},{6,0},{7,5},{8,10},{9,15},{10,... | collective-permute-start | bytes 589832 | tf_op jit(solution)/shard_map/ppermute | solution.py:26
  67.2 2.1 collective-permute-start.13
  69.3 3.5 %collective-permute-start.10 = (bf16[768,128]{1,0:T(8,128)(2,1)S(1)}, bf16[768,128]{1,0:T(8,128)(2,1)S(1)}, u32[]{:S(2)}, u32[]{:S(2)}) collective-permute-start(bf16[768,128]{1,0:T(8,128)(2,1)S(1)} %collective-permute-done.9), channel_id=1, source_target_pairs={{0,2},{1,7},{2,4},{3,1},{4,6},{5,3},{6,0},{7,5},{8,10},{9,15},{10,... | collective-permute-start | bytes 589832 | tf_op jit(solution)/shard_map/ppermute | solution.py:26
  73.0 3.0 %collective-permute-done.13 = bf16[768,128]{1,0:T(8,128)(2,1)S(1)} collective-permute-done((bf16[768,128]{1,0:T(8,128)(2,1)S(1)}, bf16[768,128]{1,0:T(8,128)(2,1)S(1)}, u32[]{:S(2)}, u32[]{:S(2)}) %collective-permute-start.13) | collective-permute-done | bytes 196640 | tf_op jit(solution)/shard_map/ppermute | solution.py:26
  75.9 1.9 collective-permute-start.14
  78.2 6.5 %collective-permute-done.14 = bf16[768,128]{1,0:T(8,128)(2,1)S(1)} collective-permute-done((bf16[768,128]{1,0:T(8,128)(2,1)S(1)}, bf16[768,128]{1,0:T(8,128)(2,1)S(1)}, u32[]{:S(2)}, u32[]{:S(2)}) %collective-permute-start.14) | collective-permute-done | bytes 196640 | tf_op jit(solution)/shard_map/ppermute | solution.py:26
  84.7 1.9 collective-permute-start.15
  87.1 0.9 copy.12
  88.0 2.3 copy.9
  90.3 1.3 multiply_convert_fusion.refs_0_
  91.6 1.9 collective-permute-start.19
  93.5 9.6 %collective-permute-done.19.refs_4_ = bf16[256,768]{1,0:T(8,128)(2,1)S(1)} collective-permute-done((bf16[256,768]{1,0:T(8,128)(2,1)S(1)}, bf16[256,768]{1,0:T(8,128)(2,1)S(1)}, u32[]{:S(2)}, u32[]{:S(2)}) %collective-permute-start.19) | collective-permute-done | bytes 393248 | tf_op jit(solution)/shard_map/ppermute | solution.py:26
  103.2 4.0 %collective-permute-start.23 = (bf16[256,768]{1,0:T(8,128)(2,1)S(1)}, bf16[256,768]{1,0:T(8,128)(2,1)S(1)}, u32[]{:S(2)}, u32[]{:S(2)}) collective-permute-start(bf16[256,768]{1,0:T(8,128)(2,1)S(1)} %collective-permute-done.19.refs_4_), channel_id=1, source_target_pairs={{0,32},{1,97},{32,64},{33,1},{64,96},{65,33},{96,0},{97,65},{2,34}... | collective-permute-start | bytes 1179656 | tf_op jit(solution)/shard_map/ppermute | solution.py:26
  107.2 10.7 %collective-permute-done.23.refs_8_ = bf16[256,768]{1,0:T(8,128)(2,1)S(1)} collective-permute-done((bf16[256,768]{1,0:T(8,128)(2,1)S(1)}, bf16[256,768]{1,0:T(8,128)(2,1)S(1)}, u32[]{:S(2)}, u32[]{:S(2)}) %collective-permute-start.23) | collective-permute-done | bytes 393248 | tf_op jit(solution)/shard_map/ppermute | solution.py:26
  117.9 2.8 %collective-permute-start.27 = (bf16[256,768]{1,0:T(8,128)(2,1)S(1)}, bf16[256,768]{1,0:T(8,128)(2,1)S(1)}, u32[]{:S(2)}, u32[]{:S(2)}) collective-permute-start(bf16[256,768]{1,0:T(8,128)(2,1)S(1)} %collective-permute-done.23.refs_8_), channel_id=1, source_target_pairs={{0,32},{1,97},{32,64},{33,1},{64,96},{65,33},{96,0},{97,65},{2,34}... | collective-permute-start | bytes 1179656 | tf_op jit(solution)/shard_map/ppermute | solution.py:26
  120.7 3.4 %collective-permute-start.16 = (bf16[256,768]{1,0:T(8,128)(2,1)S(1)}, bf16[256,768]{1,0:T(8,128)(2,1)S(1)}, u32[]{:S(2)}, u32[]{:S(2)}) collective-permute-start(bf16[256,768]{1,0:T(8,128)(2,1)S(1)} %multiply_convert_fusion.refs_0_), channel_id=1, source_target_pairs={{0,128},{1,385},{128,256},{129,1},{256,384},{257,129},{384,0},{385... | collective-permute-start | bytes 1179656 | tf_op jit(solution)/shard_map/ppermute | solution.py:26
  124.1 3.1 %collective-permute-start.20 = (bf16[256,768]{1,0:T(8,128)(2,1)S(1)}, bf16[256,768]{1,0:T(8,128)(2,1)S(1)}, u32[]{:S(2)}, u32[]{:S(2)}) collective-permute-start(bf16[256,768]{1,0:T(8,128)(2,1)S(1)} %collective-permute-done.19.refs_4_), channel_id=1, source_target_pairs={{0,128},{1,385},{128,256},{129,1},{256,384},{257,129},{384,0},{385... | collective-permute-start | bytes 1179656 | tf_op jit(solution)/shard_map/ppermute | solution.py:26
  127.2 0.8 copy-done.2
  128.0 2.4 collective-permute-start.24
  131.1 0.9 collective-permute-done.27.refs_12_
  131.9 3.4 %collective-permute-start.28 = (bf16[256,768]{1,0:T(8,128)(2,1)S(1)}, bf16[256,768]{1,0:T(8,128)(2,1)S(1)}, u32[]{:S(2)}, u32[]{:S(2)}) collective-permute-start(bf16[256,768]{1,0:T(8,128)(2,1)S(1)} %collective-permute-done.27.refs_12_), channel_id=1, source_target_pairs={{0,128},{1,385},{128,256},{129,1},{256,384},{257,129},{384,0},{385... | collective-permute-start | bytes 1179656 | tf_op jit(solution)/shard_map/ppermute | solution.py:26
  136.1 3.1 %collective-permute-start.17 = (bf16[256,768]{1,0:T(8,128)(2,1)S(1)}, bf16[256,768]{1,0:T(8,128)(2,1)}, u32[]{:S(2)}, u32[]{:S(2)}) collective-permute-start(bf16[256,768]{1,0:T(8,128)(2,1)S(1)} %collective-permute-done.16.refs_1_), channel_id=1, source_target_pairs={{0,128},{1,385},{128,256},{129,1},{256,384},{257,129},{384,0},{385... | collective-permute-start | bytes 1179656 | tf_op jit(solution)/shard_map/ppermute | solution.py:26
  139.2 0.7 copy-done.8
  139.9 2.5 collective-permute-start.21
  142.5 0.8 copy-done.10
  143.3 3.2 %collective-permute-start.25 = (bf16[256,768]{1,0:T(8,128)(2,1)S(1)}, bf16[256,768]{1,0:T(8,128)(2,1)}, u32[]{:S(2)}, u32[]{:S(2)}) collective-permute-start(bf16[256,768]{1,0:T(8,128)(2,1)S(1)} %collective-permute-done.24.refs_9_), channel_id=1, source_target_pairs={{0,128},{1,385},{128,256},{129,1},{256,384},{257,129},{384,0},{385... | collective-permute-start | bytes 1179656 | tf_op jit(solution)/shard_map/ppermute | solution.py:26
  146.5 0.8 copy-done.12
  147.3 3.4 %collective-permute-start.29 = (bf16[256,768]{1,0:T(8,128)(2,1)S(1)}, bf16[256,768]{1,0:T(8,128)(2,1)}, u32[]{:S(2)}, u32[]{:S(2)}) collective-permute-start(bf16[256,768]{1,0:T(8,128)(2,1)S(1)} %collective-permute-done.28.refs_13_), channel_id=1, source_target_pairs={{0,128},{1,385},{128,256},{129,1},{256,384},{257,129},{384,0},{385... | collective-permute-start | bytes 1179656 | tf_op jit(solution)/shard_map/ppermute | solution.py:26
  150.7 0.8 copy-done.14
  151.5 3.1 %collective-permute-start.18 = (bf16[256,768]{1,0:T(8,128)(2,1)}, bf16[256,768]{1,0:T(8,128)(2,1)}, u32[]{:S(2)}, u32[]{:S(2)}) collective-permute-start(bf16[256,768]{1,0:T(8,128)(2,1)} %collective-permute-done.17.refs_2_), channel_id=1, source_target_pairs={{0,128},{1,385},{128,256},{129,1},{256,384},{257,129},{384,0},{385... | collective-permute-start | bytes 1179656 | tf_op jit(solution)/shard_map/ppermute | solution.py:26
  154.6 2.6 collective-permute-start.22
  157.2 3.2 %collective-permute-start.26 = (bf16[256,768]{1,0:T(8,128)(2,1)}, bf16[256,768]{1,0:T(8,128)(2,1)}, u32[]{:S(2)}, u32[]{:S(2)}) collective-permute-start(bf16[256,768]{1,0:T(8,128)(2,1)} %collective-permute-done.25.refs_10_), channel_id=1, source_target_pairs={{0,128},{1,385},{128,256},{129,1},{256,384},{257,129},{384,0},{385... | collective-permute-start | bytes 1179656 | tf_op jit(solution)/shard_map/ppermute | solution.py:26
  160.4 3.4 %collective-permute-start.30 = (bf16[256,768]{1,0:T(8,128)(2,1)}, bf16[256,768]{1,0:T(8,128)(2,1)}, u32[]{:S(2)}, u32[]{:S(2)}) collective-permute-start(bf16[256,768]{1,0:T(8,128)(2,1)} %collective-permute-done.29.refs_14_), channel_id=1, source_target_pairs={{0,128},{1,385},{128,256},{129,1},{256,384},{257,129},{384,0},{385... | collective-permute-start | bytes 1179656 | tf_op jit(solution)/shard_map/ppermute | solution.py:26
  164.4 4.0 %collective-permute-done.22.refs_7_ = bf16[256,768]{1,0:T(8,128)(2,1)} collective-permute-done((bf16[256,768]{1,0:T(8,128)(2,1)}, bf16[256,768]{1,0:T(8,128)(2,1)}, u32[]{:S(2)}, u32[]{:S(2)}) %collective-permute-start.22) | collective-permute-done | bytes 393248 | tf_op jit(solution)/shard_map/ppermute | solution.py:26
  168.4 4.2 %collective-permute-done.26.refs_11_ = bf16[256,768]{1,0:T(8,128)(2,1)} collective-permute-done((bf16[256,768]{1,0:T(8,128)(2,1)}, bf16[256,768]{1,0:T(8,128)(2,1)}, u32[]{:S(2)}, u32[]{:S(2)}) %collective-permute-start.26) | collective-permute-done | bytes 393248 | tf_op jit(solution)/shard_map/ppermute | solution.py:26
  172.6 4.2 %collective-permute-done.30.refs_15_ = bf16[256,768]{1,0:T(8,128)(2,1)} collective-permute-done((bf16[256,768]{1,0:T(8,128)(2,1)}, bf16[256,768]{1,0:T(8,128)(2,1)}, u32[]{:S(2)}, u32[]{:S(2)}) %collective-permute-start.30) | collective-permute-done | bytes 393248 | tf_op jit(solution)/shard_map/ppermute | solution.py:26
  176.8 1.0 copy-done.3
  177.8 1.0 copy-done.5
  178.8 1.0 copy-done.7
  179.8 1.0 copy-done.9
  180.8 1.0 copy-done.11
  181.8 1.0 copy-done.13
  182.8 1.0 copy-done.15
  183.8 9.8 %shard_map.73 = (f32[768,768]{1,0:T(8,128)S(1)}, f32[768,1]{1,0:T(8,128)S(1)}) custom-call(s32[48]{0:T(128)S(1)} %stack.246.place_ref, s32[6,6]{1,0:T(8,128)S(1)} %copy-done.17, bf16[16,768,128]{2,1,0:T(8,128)(2,1)S(1)} %bitcast_dynamic-update-slice_fusion.own_ref, bf16[16,768,128]{2,1,0:T(8,128)(2,1)} %collective-permute-done.15.other_ref, ...), custom_call_target="tpu_custom_call" | custom-call | tf_op jit(solution)/shard_map/pallas_call | solution.py:94
  193.6 1.4 copy-done
  195.0 0.7 copy-done.16
  195.7 5.6 %psum.21 = f32[768,1]{1,0:T(8,128)S(1)} all-reduce(f32[768,1]{1,0:T(8,128)} %copy-done.16), channel_id=1, replica_groups=mesh['x'=4,'zl'=4,'zh'=4,'y'=4,'core'=2] {'core'}, use_global_device_ids=true, to_apply=%region_0.1 | all-reduce | flops 768 | bytes 6144 | tf_op jit(solution)/shard_map/psum | solution.py:112
  201.3 18.5 %psum.22 = f32[768,1]{1,0:T(8,128)S(1)} all-reduce(f32[768,1]{1,0:T(8,128)S(1)} %psum.21), channel_id=1, replica_groups=mesh['x'=4,'zl'=4,'zh'=4,'y'=4,'core'=2] {'y'}, use_global_device_ids=true, to_apply=%region_1.2 | all-reduce | flops 768 | bytes 6144 | tf_op jit(solution)/shard_map/psum | solution.py:112
  219.9 40.8 %psum.23 = f32[768,1]{1,0:T(8,128)S(1)} all-reduce(f32[768,1]{1,0:T(8,128)S(1)} %psum.22), channel_id=1, replica_groups=mesh['x'=4,'zl'=4,'zh'=4,'y'=4,'core'=2] {'zh'}, use_global_device_ids=true, to_apply=%region_2.3 | all-reduce | flops 768 | bytes 6144 | tf_op jit(solution)/shard_map/psum | solution.py:112
  260.8 1.7 multiply_divide_fusion
  (69 shorter events, 3.6 us)
Async XLA Ops:
  0.7 85.9 %copy-start.18 = (f32[2,6]{1,0:T(2,128)S(1)}, f32[2,6]{1,0:T(2,128)}, u32[]{:S(2)}) copy-start(f32[2,6]{1,0:T(2,128)} %param.11) | copy-start | bytes 148
  0.8 85.9 %copy-start.19 = (s32[2,6]{1,0:T(2,128)S(1)}, s32[2,6]{1,0:T(2,128)}, u32[]{:S(2)}) copy-start(s32[2,6]{1,0:T(2,128)} %param.12) | copy-start | bytes 148
  1.9 16.7 %collective-permute-start.3 = (bf16[768,128]{1,0:T(8,128)(2,1)S(1)}, bf16[768,128]{1,0:T(8,128)(2,1)S(1)}, u32[]{:S(2)}, u32[]{:S(2)}) collective-permute-start(bf16[768,128]{1,0:T(8,128)(2,1)S(1)} %get-tuple-element.10), channel_id=1, source_target_pairs={{0,8},{1,25},{8,16},{9,1},{16,24},{17,9},{24,0},{25,17},{2,10},{3,... | collective-permute-start | bytes 589832 | tf_op jit(solution)/shard_map/ppermute | solution.py:26
  11.0 21.9 %collective-permute-start = (bf16[768,128]{1,0:T(8,128)(2,1)S(1)}, bf16[768,128]{1,0:T(8,128)(2,1)S(1)}, u32[]{:S(2)}, u32[]{:S(2)}) collective-permute-start(bf16[768,128]{1,0:T(8,128)(2,1)S(1)} %get-tuple-element.10), channel_id=1, source_target_pairs={{0,2},{1,7},{2,4},{3,1},{4,6},{5,3},{6,0},{7,5},{8,10},{9,15},{10,... | collective-permute-start | bytes 589832 | tf_op jit(solution)/shard_map/ppermute | solution.py:26
  18.6 17.8 %collective-permute-start.7 = (bf16[768,128]{1,0:T(8,128)(2,1)S(1)}, bf16[768,128]{1,0:T(8,128)(2,1)S(1)}, u32[]{:S(2)}, u32[]{:S(2)}) collective-permute-start(bf16[768,128]{1,0:T(8,128)(2,1)S(1)} %collective-permute-done.3), channel_id=1, source_target_pairs={{0,8},{1,25},{8,16},{9,1},{16,24},{17,9},{24,0},{25,17},{2,10},{3,... | collective-permute-start | bytes 589832 | tf_op jit(solution)/shard_map/ppermute | solution.py:26
  29.3 21.2 %collective-permute-start.4 = (bf16[768,128]{1,0:T(8,128)(2,1)S(1)}, bf16[768,128]{1,0:T(8,128)(2,1)S(1)}, u32[]{:S(2)}, u32[]{:S(2)}) collective-permute-start(bf16[768,128]{1,0:T(8,128)(2,1)S(1)} %collective-permute-done.3), channel_id=1, source_target_pairs={{0,2},{1,7},{2,4},{3,1},{4,6},{5,3},{6,0},{7,5},{8,10},{9,15},{10,... | collective-permute-start | bytes 589832 | tf_op jit(solution)/shard_map/ppermute | solution.py:26
  32.8 15.0 %collective-permute-start.1 = (bf16[768,128]{1,0:T(8,128)(2,1)S(1)}, bf16[768,128]{1,0:T(8,128)(2,1)S(1)}, u32[]{:S(2)}, u32[]{:S(2)}) collective-permute-start(bf16[768,128]{1,0:T(8,128)(2,1)S(1)} %collective-permute-done), channel_id=1, source_target_pairs={{0,2},{1,7},{2,4},{3,1},{4,6},{5,3},{6,0},{7,5},{8,10},{9,15},{10,... | collective-permute-start | bytes 589832 | tf_op jit(solution)/shard_map/ppermute | solution.py:26
  36.4 20.4 %collective-permute-start.11 = (bf16[768,128]{1,0:T(8,128)(2,1)S(1)}, bf16[768,128]{1,0:T(8,128)(2,1)S(1)}, u32[]{:S(2)}, u32[]{:S(2)}) collective-permute-start(bf16[768,128]{1,0:T(8,128)(2,1)S(1)} %collective-permute-done.7), channel_id=1, source_target_pairs={{0,8},{1,25},{8,16},{9,1},{16,24},{17,9},{24,0},{25,17},{2,10},{3,... | collective-permute-start | bytes 589832 | tf_op jit(solution)/shard_map/ppermute | solution.py:26
  44.7 15.7 %collective-permute-start.8 = (bf16[768,128]{1,0:T(8,128)(2,1)S(1)}, bf16[768,128]{1,0:T(8,128)(2,1)S(1)}, u32[]{:S(2)}, u32[]{:S(2)}) collective-permute-start(bf16[768,128]{1,0:T(8,128)(2,1)S(1)} %collective-permute-done.7), channel_id=1, source_target_pairs={{0,2},{1,7},{2,4},{3,1},{4,6},{5,3},{6,0},{7,5},{8,10},{9,15},{10,... | collective-permute-start | bytes 589832 | tf_op jit(solution)/shard_map/ppermute | solution.py:26
  47.9 12.4 %collective-permute-start.2 = (bf16[768,128]{1,0:T(8,128)(2,1)S(1)}, bf16[768,128]{1,0:T(8,128)(2,1)S(1)}, u32[]{:S(2)}, u32[]{:S(2)}) collective-permute-start(bf16[768,128]{1,0:T(8,128)(2,1)S(1)} %collective-permute-done.1), channel_id=1, source_target_pairs={{0,2},{1,7},{2,4},{3,1},{4,6},{5,3},{6,0},{7,5},{8,10},{9,15},{10,... | collective-permute-start | bytes 589832 | tf_op jit(solution)/shard_map/ppermute | solution.py:26
  50.5 13.4 %collective-permute-start.5 = (bf16[768,128]{1,0:T(8,128)(2,1)S(1)}, bf16[768,128]{1,0:T(8,128)(2,1)S(1)}, u32[]{:S(2)}, u32[]{:S(2)}) collective-permute-start(bf16[768,128]{1,0:T(8,128)(2,1)S(1)} %collective-permute-done.4), channel_id=1, source_target_pairs={{0,2},{1,7},{2,4},{3,1},{4,6},{5,3},{6,0},{7,5},{8,10},{9,15},{10,... | collective-permute-start | bytes 589832 | tf_op jit(solution)/shard_map/ppermute | solution.py:26
  56.8 10.3 %collective-permute-start.12 = (bf16[768,128]{1,0:T(8,128)(2,1)S(1)}, bf16[768,128]{1,0:T(8,128)(2,1)S(1)}, u32[]{:S(2)}, u32[]{:S(2)}) collective-permute-start(bf16[768,128]{1,0:T(8,128)(2,1)S(1)} %collective-permute-done.11), channel_id=1, source_target_pairs={{0,2},{1,7},{2,4},{3,1},{4,6},{5,3},{6,0},{7,5},{8,10},{9,15},{10,... | collective-permute-start | bytes 589832 | tf_op jit(solution)/shard_map/ppermute | solution.py:26
  60.4 8.9 %collective-permute-start.9 = (bf16[768,128]{1,0:T(8,128)(2,1)S(1)}, bf16[768,128]{1,0:T(8,128)(2,1)S(1)}, u32[]{:S(2)}, u32[]{:S(2)}) collective-permute-start(bf16[768,128]{1,0:T(8,128)(2,1)S(1)} %collective-permute-done.8), channel_id=1, source_target_pairs={{0,2},{1,7},{2,4},{3,1},{4,6},{5,3},{6,0},{7,5},{8,10},{9,15},{10,... | collective-permute-start | bytes 589832 | tf_op jit(solution)/shard_map/ppermute | solution.py:26
  63.9 8.9 %collective-permute-start.6 = (bf16[768,128]{1,0:T(8,128)(2,1)S(1)}, bf16[768,128]{1,0:T(8,128)(2,1)S(1)}, u32[]{:S(2)}, u32[]{:S(2)}) collective-permute-start(bf16[768,128]{1,0:T(8,128)(2,1)S(1)} %collective-permute-done.5), channel_id=1, source_target_pairs={{0,2},{1,7},{2,4},{3,1},{4,6},{5,3},{6,0},{7,5},{8,10},{9,15},{10,... | collective-permute-start | bytes 589832 | tf_op jit(solution)/shard_map/ppermute | solution.py:26
  67.2 8.8 %collective-permute-start.13 = (bf16[768,128]{1,0:T(8,128)(2,1)S(1)}, bf16[768,128]{1,0:T(8,128)(2,1)S(1)}, u32[]{:S(2)}, u32[]{:S(2)}) collective-permute-start(bf16[768,128]{1,0:T(8,128)(2,1)S(1)} %collective-permute-done.12), channel_id=1, source_target_pairs={{0,2},{1,7},{2,4},{3,1},{4,6},{5,3},{6,0},{7,5},{8,10},{9,15},{10,... | collective-permute-start | bytes 589832 | tf_op jit(solution)/shard_map/ppermute | solution.py:26
  69.3 8.8 %collective-permute-start.10 = (bf16[768,128]{1,0:T(8,128)(2,1)S(1)}, bf16[768,128]{1,0:T(8,128)(2,1)S(1)}, u32[]{:S(2)}, u32[]{:S(2)}) collective-permute-start(bf16[768,128]{1,0:T(8,128)(2,1)S(1)} %collective-permute-done.9), channel_id=1, source_target_pairs={{0,2},{1,7},{2,4},{3,1},{4,6},{5,3},{6,0},{7,5},{8,10},{9,15},{10,... | collective-permute-start | bytes 589832 | tf_op jit(solution)/shard_map/ppermute | solution.py:26
  75.9 8.8 %collective-permute-start.14 = (bf16[768,128]{1,0:T(8,128)(2,1)S(1)}, bf16[768,128]{1,0:T(8,128)(2,1)S(1)}, u32[]{:S(2)}, u32[]{:S(2)}) collective-permute-start(bf16[768,128]{1,0:T(8,128)(2,1)S(1)} %collective-permute-done.13), channel_id=1, source_target_pairs={{0,2},{1,7},{2,4},{3,1},{4,6},{5,3},{6,0},{7,5},{8,10},{9,15},{10,... | collective-permute-start | bytes 589832 | tf_op jit(solution)/shard_map/ppermute | solution.py:26
  84.7 92.1 %collective-permute-start.15 = (bf16[16,768,128]{2,1,0:T(8,128)(2,1)S(1)}, bf16[16,768,128]{2,1,0:T(8,128)(2,1)}, u32[]{:S(2)}, u32[]{:S(2)}) collective-permute-start(bf16[16,768,128]{2,1,0:T(8,128)(2,1)S(1)} %bitcast_dynamic-update-slice_fusion.own_ref), channel_id=1, source_target_pairs={{0,1},{1,0},{2,3},{3,2},{4,5},{5,4},{6,7},{7,6},{8,9},{9,8},{10,11... | collective-permute-start | bytes 9437192 | tf_op jit(solution)/shard_map/ppermute | solution.py:86
  86.8 90.0 %copy-start.17 = (s32[6,6]{1,0:T(8,128)S(1)}, s32[6,6]{1,0:T(8,128)}, u32[]{:S(2)}) copy-start(s32[6,6]{1,0:T(8,128)} %keep_ref.1) | copy-start | bytes 436
  91.6 11.6 %collective-permute-start.19 = (bf16[256,768]{1,0:T(8,128)(2,1)S(1)}, bf16[256,768]{1,0:T(8,128)(2,1)S(1)}, u32[]{:S(2)}, u32[]{:S(2)}) collective-permute-start(bf16[256,768]{1,0:T(8,128)(2,1)S(1)} %multiply_convert_fusion.refs_0_), channel_id=1, source_target_pairs={{0,32},{1,97},{32,64},{33,1},{64,96},{65,33},{96,0},{97,65},{2,34}... | collective-permute-start | bytes 1179656 | tf_op jit(solution)/shard_map/ppermute | solution.py:26
  103.2 14.7 %collective-permute-start.23 = (bf16[256,768]{1,0:T(8,128)(2,1)S(1)}, bf16[256,768]{1,0:T(8,128)(2,1)S(1)}, u32[]{:S(2)}, u32[]{:S(2)}) collective-permute-start(bf16[256,768]{1,0:T(8,128)(2,1)S(1)} %collective-permute-done.19.refs_4_), channel_id=1, source_target_pairs={{0,32},{1,97},{32,64},{33,1},{64,96},{65,33},{96,0},{97,65},{2,34}... | collective-permute-start | bytes 1179656 | tf_op jit(solution)/shard_map/ppermute | solution.py:26
  117.9 14.1 %collective-permute-start.27 = (bf16[256,768]{1,0:T(8,128)(2,1)S(1)}, bf16[256,768]{1,0:T(8,128)(2,1)S(1)}, u32[]{:S(2)}, u32[]{:S(2)}) collective-permute-start(bf16[256,768]{1,0:T(8,128)(2,1)S(1)} %collective-permute-done.23.refs_8_), channel_id=1, source_target_pairs={{0,32},{1,97},{32,64},{33,1},{64,96},{65,33},{96,0},{97,65},{2,34}... | collective-permute-start | bytes 1179656 | tf_op jit(solution)/shard_map/ppermute | solution.py:26
  120.7 15.4 %collective-permute-start.16 = (bf16[256,768]{1,0:T(8,128)(2,1)S(1)}, bf16[256,768]{1,0:T(8,128)(2,1)S(1)}, u32[]{:S(2)}, u32[]{:S(2)}) collective-permute-start(bf16[256,768]{1,0:T(8,128)(2,1)S(1)} %multiply_convert_fusion.refs_0_), channel_id=1, source_target_pairs={{0,128},{1,385},{128,256},{129,1},{256,384},{257,129},{384,0},{385... | collective-permute-start | bytes 1179656 | tf_op jit(solution)/shard_map/ppermute | solution.py:26
  124.1 15.8 %collective-permute-start.20 = (bf16[256,768]{1,0:T(8,128)(2,1)S(1)}, bf16[256,768]{1,0:T(8,128)(2,1)S(1)}, u32[]{:S(2)}, u32[]{:S(2)}) collective-permute-start(bf16[256,768]{1,0:T(8,128)(2,1)S(1)} %collective-permute-done.19.refs_4_), channel_id=1, source_target_pairs={{0,128},{1,385},{128,256},{129,1},{256,384},{257,129},{384,0},{385... | collective-permute-start | bytes 1179656 | tf_op jit(solution)/shard_map/ppermute | solution.py:26
  127.2 0.8 copy-start.2
  128.0 15.3 %collective-permute-start.24 = (bf16[256,768]{1,0:T(8,128)(2,1)S(1)}, bf16[256,768]{1,0:T(8,128)(2,1)S(1)}, u32[]{:S(2)}, u32[]{:S(2)}) collective-permute-start(bf16[256,768]{1,0:T(8,128)(2,1)S(1)} %collective-permute-done.23.refs_8_), channel_id=1, source_target_pairs={{0,128},{1,385},{128,256},{129,1},{256,384},{257,129},{384,0},{385... | collective-permute-start | bytes 1179656 | tf_op jit(solution)/shard_map/ppermute | solution.py:26
  130.4 0.7 copy-start.4
  131.9 15.4 %collective-permute-start.28 = (bf16[256,768]{1,0:T(8,128)(2,1)S(1)}, bf16[256,768]{1,0:T(8,128)(2,1)S(1)}, u32[]{:S(2)}, u32[]{:S(2)}) collective-permute-start(bf16[256,768]{1,0:T(8,128)(2,1)S(1)} %collective-permute-done.27.refs_12_), channel_id=1, source_target_pairs={{0,128},{1,385},{128,256},{129,1},{256,384},{257,129},{384,0},{385... | collective-permute-start | bytes 1179656 | tf_op jit(solution)/shard_map/ppermute | solution.py:26
  135.3 0.7 copy-start.6
  136.1 15.4 %collective-permute-start.17 = (bf16[256,768]{1,0:T(8,128)(2,1)S(1)}, bf16[256,768]{1,0:T(8,128)(2,1)}, u32[]{:S(2)}, u32[]{:S(2)}) collective-permute-start(bf16[256,768]{1,0:T(8,128)(2,1)S(1)} %collective-permute-done.16.refs_1_), channel_id=1, source_target_pairs={{0,128},{1,385},{128,256},{129,1},{256,384},{257,129},{384,0},{385... | collective-permute-start | bytes 1179656 | tf_op jit(solution)/shard_map/ppermute | solution.py:26
  139.2 0.7 copy-start.8
  139.9 14.7 %collective-permute-start.21 = (bf16[256,768]{1,0:T(8,128)(2,1)S(1)}, bf16[256,768]{1,0:T(8,128)(2,1)}, u32[]{:S(2)}, u32[]{:S(2)}) collective-permute-start(bf16[256,768]{1,0:T(8,128)(2,1)S(1)} %collective-permute-done.20.refs_5_), channel_id=1, source_target_pairs={{0,128},{1,385},{128,256},{129,1},{256,384},{257,129},{384,0},{385... | collective-permute-start | bytes 1179656 | tf_op jit(solution)/shard_map/ppermute | solution.py:26
  142.5 0.8 copy-start.10
  143.3 13.9 %collective-permute-start.25 = (bf16[256,768]{1,0:T(8,128)(2,1)S(1)}, bf16[256,768]{1,0:T(8,128)(2,1)}, u32[]{:S(2)}, u32[]{:S(2)}) collective-permute-start(bf16[256,768]{1,0:T(8,128)(2,1)S(1)} %collective-permute-done.24.refs_9_), channel_id=1, source_target_pairs={{0,128},{1,385},{128,256},{129,1},{256,384},{257,129},{384,0},{385... | collective-permute-start | bytes 1179656 | tf_op jit(solution)/shard_map/ppermute | solution.py:26
  146.5 0.8 copy-start.12
  147.3 13.1 %collective-permute-start.29 = (bf16[256,768]{1,0:T(8,128)(2,1)S(1)}, bf16[256,768]{1,0:T(8,128)(2,1)}, u32[]{:S(2)}, u32[]{:S(2)}) collective-permute-start(bf16[256,768]{1,0:T(8,128)(2,1)S(1)} %collective-permute-done.28.refs_13_), channel_id=1, source_target_pairs={{0,128},{1,385},{128,256},{129,1},{256,384},{257,129},{384,0},{385... | collective-permute-start | bytes 1179656 | tf_op jit(solution)/shard_map/ppermute | solution.py:26
  150.7 0.8 copy-start.14
  151.5 12.9 %collective-permute-start.18 = (bf16[256,768]{1,0:T(8,128)(2,1)}, bf16[256,768]{1,0:T(8,128)(2,1)}, u32[]{:S(2)}, u32[]{:S(2)}) collective-permute-start(bf16[256,768]{1,0:T(8,128)(2,1)} %collective-permute-done.17.refs_2_), channel_id=1, source_target_pairs={{0,128},{1,385},{128,256},{129,1},{256,384},{257,129},{384,0},{385... | collective-permute-start | bytes 1179656 | tf_op jit(solution)/shard_map/ppermute | solution.py:26
  154.6 13.8 %collective-permute-start.22 = (bf16[256,768]{1,0:T(8,128)(2,1)}, bf16[256,768]{1,0:T(8,128)(2,1)}, u32[]{:S(2)}, u32[]{:S(2)}) collective-permute-start(bf16[256,768]{1,0:T(8,128)(2,1)} %collective-permute-done.21.refs_6_), channel_id=1, source_target_pairs={{0,128},{1,385},{128,256},{129,1},{256,384},{257,129},{384,0},{385... | collective-permute-start | bytes 1179656 | tf_op jit(solution)/shard_map/ppermute | solution.py:26
  157.2 15.4 %collective-permute-start.26 = (bf16[256,768]{1,0:T(8,128)(2,1)}, bf16[256,768]{1,0:T(8,128)(2,1)}, u32[]{:S(2)}, u32[]{:S(2)}) collective-permute-start(bf16[256,768]{1,0:T(8,128)(2,1)} %collective-permute-done.25.refs_10_), channel_id=1, source_target_pairs={{0,128},{1,385},{128,256},{129,1},{256,384},{257,129},{384,0},{385... | collective-permute-start | bytes 1179656 | tf_op jit(solution)/shard_map/ppermute | solution.py:26
  160.4 16.4 %collective-permute-start.30 = (bf16[256,768]{1,0:T(8,128)(2,1)}, bf16[256,768]{1,0:T(8,128)(2,1)}, u32[]{:S(2)}, u32[]{:S(2)}) collective-permute-start(bf16[256,768]{1,0:T(8,128)(2,1)} %collective-permute-done.29.refs_14_), channel_id=1, source_target_pairs={{0,128},{1,385},{128,256},{129,1},{256,384},{257,129},{384,0},{385... | collective-permute-start | bytes 1179656 | tf_op jit(solution)/shard_map/ppermute | solution.py:26
  176.8 1.0 copy-start.3
  177.8 1.0 copy-start.5
  178.8 1.0 copy-start.7
  179.8 1.0 copy-start.9
  180.8 1.0 copy-start.11
  181.8 1.0 copy-start.13
  182.8 1.0 copy-start.15
  193.6 1.4 copy-start
  195.0 0.7 copy-start.16
  195.7 65.1 %copy-start.1 = (f32[768,768]{1,0:T(8,128)S(1)}, f32[768,768]{1,0:T(8,128)}, u32[]{:S(2)}) copy-start(f32[768,768]{1,0:T(8,128)} %copy-done) | copy-start | bytes 7077892

commit v2 on v0

v2 whole, which is shorter than its diff:
```python
import functools

import jax
import jax.numpy as jnp
from jax import lax
from jax.experimental import pallas as pl
from jax.experimental.pallas import tpu as pltpu
from jax.sharding import Mesh, PartitionSpec as P

AXES = ("x", "zl", "zh", "y", "core")
SIDE = 4
TILE = 128
MIB = 1024 * 1024
VMEM = pl.BlockSpec(memory_space=pltpu.VMEM)
SMEM = pl.BlockSpec(memory_space=pltpu.SMEM)
ANY = pl.BlockSpec(memory_space=pl.ANY)


def step(value, axis, by=1):
    pairs = []
    for i in range(SIDE):
        pairs.append((2 * i, 2 * ((i + by) % SIDE)))
        pairs.append((2 * i + 1, 2 * ((i - by) % SIDE) + 1))
    return lax.ppermute(value, (axis, "core"), pairs)


def swap(value):
    return lax.ppermute(value, "core", [(0, 1), (1, 0)])


def copy_parts(count, *refs):
    at = 0
    for ref in refs[:count]:
        refs[-1][at:at + ref.shape[0]] = ref[...]
        at += ref.shape[0]


def join(parts, after=()):
    shape = (sum(p.shape[0] for p in parts),) + parts[0].shape[1:]
    return pl.pallas_call(
        functools.partial(copy_parts, len(parts)),
        out_shape=jax.ShapeDtypeStruct(shape, jnp.bfloat16),
        in_specs=[VMEM] * (len(parts) + len(after)),
        out_specs=VMEM,
        compiler_params=pltpu.CompilerParams(vmem_limit_bytes=8 * MIB),
    )(*parts, *after)


def scale_tiles(*refs):
    given, made, held, sems = refs[:6], refs[6:8], refs[8:14], refs[14]
    copies = [pltpu.make_async_copy(given[i], held[i], sems.at[i]) for i in range(6)]
    for copy in copies:
        copy.start()
    for side in range(2):
        for copy in copies[3 * side:3 * side + 3]:
            copy.wait()
        scale_ref, keep_ref, values_ref = held[3 * side:3 * side + 3]
        factors = scale_ref[...] * keep_ref[...].astype(jnp.float32)
        rows, cols = (n // TILE for n in values_ref.shape)
        for i in range(rows):
            for j in range(cols):
                at = (slice(i * TILE, (i + 1) * TILE), slice(j * TILE, (j + 1) * TILE))
                factor = factors[i:i + 1, j:j + 1] if cols > 1 else factors[0:1, i:i + 1]
                made[side][at] = (values_ref[at].astype(jnp.float32) * factor).astype(jnp.bfloat16)


def tiled(*operands):
    return pl.pallas_call(
        scale_tiles,
        out_shape=[jax.ShapeDtypeStruct(operands[i].shape, jnp.bfloat16) for i in (2, 5)],
        in_specs=[pl.BlockSpec(memory_space=pl.ANY)] * 6,
        out_specs=[VMEM] * 2,
        scratch_shapes=[pltpu.VMEM(v.shape, v.dtype) for v in operands] + [pltpu.SemaphoreType.DMA((6,))],
        compiler_params=pltpu.CompilerParams(vmem_limit_bytes=60 * MIB),
    )(*operands)


def multiply(left_at, right_at, at_ref, keep_ref, *refs):
    left_refs, refs = refs[:len(left_at)], refs[len(left_at):]
    right_refs, refs = refs[:len(right_at)], refs[len(right_at):]
    pruned_ref, total_ref, left, right = refs
    x, zl, zh, y, core = (at_ref[i] for i in range(5))
    way = 1 - 2 * core

    def left_place(first, lanes, first_step, sign, i):
        k, s = first + lax.rem(i, lanes), first_step + lax.div(i, lanes)
        block = lax.rem(zh - k * sign * way + SIDE, SIDE) * SIDE + lax.rem(y - s * sign * way + SIDE, SIDE)
        return block * 2 + (core if sign > 0 else 1 - core)

    def right_place(first, lanes, first_step, i):
        k, s = first + lax.rem(i, lanes), first_step + lax.div(i, lanes)
        return lax.rem(x - s * way + SIDE, SIDE) * SIDE + lax.rem(zl - k * way + SIDE, SIDE)

    for held, place, places, given in ((left, left_place, left_at, left_refs), (right, right_place, right_at, right_refs)):
        for ref, at in zip(given, places):
            def put(i, carry, held=held, place=place, ref=ref, at=at):
                held[place(*at, i)] = ref[i]
                return carry

            lax.fori_loop(0, ref.shape[0], put, 0)
    blocks, rows = left.shape[0], 2 * TILE
    cols = right.shape[2]
    for m in range(left.shape[1] // rows):
        lhs = jnp.concatenate([left[k, m * rows:(m + 1) * rows, :] for k in range(blocks)], axis=1)
        product = jnp.dot(lhs, right[...].reshape(blocks * TILE, cols), preferred_element_type=jnp.float32)
        for r in range(rows // TILE):
            total = jnp.zeros((TILE, TILE), jnp.float32)
            i = m * (rows // TILE) + r
            for n in range(cols // TILE):
                block = product[r * TILE:(r + 1) * TILE, n * TILE:(n + 1) * TILE]
                block = block * block * keep_ref[i, n].astype(jnp.float32)
                pruned_ref[i * TILE:(i + 1) * TILE, n * TILE:(n + 1) * TILE] = block
                total = total + block
            total_ref[i:i + 1, :] = jnp.sum(total.T, axis=0, keepdims=True)


def per_device(left_vals, left_scale, left_keep, right_vals, right_scale, right_keep, result_keep):
    at = jnp.stack([lax.axis_index(a) for a in AXES]).astype(jnp.int32)
    rows, cols = left_vals.shape[0], right_vals.shape[1]
    right_tiles, left_tiles = tiled(
        right_scale, right_keep, right_vals, left_scale.reshape(1, -1), left_keep.reshape(1, -1), left_vals
    )
    z0, h0 = right_tiles[None], left_tiles[None]

    high, lane = [h0], [z0]
    for _ in range(SIDE - 1):
        high.append(step(high[-1], "zh"))
        lane.append(step(lane[-1], "zl"))
    lefts, rights = [], []
    for first in (0, 2):
        own = [join(high[first:first + 2])]
        for _ in range(SIDE - 1):
            own.append(step(own[-1], "y"))
        own = join(own)
        lefts.append((own, (first, 2, 0, 1)))
        lefts.append((swap(own), (first, 2, 0, -1)))
    for first in (0, 2):
        block = join(lane[first:first + 2])
        rights.append((block, (first, 2, 0)))
        for s in range(1, SIDE):
            block = step(block, "x")
            rights.append((block, (first, 2, s)))
    operands = [v for v, _ in lefts + rights]
    pruned, totals = pl.pallas_call(
        functools.partial(multiply, [p for _, p in lefts], [p for _, p in rights]),
        out_shape=(
            jax.ShapeDtypeStruct((rows, cols), jnp.float32),
            jax.ShapeDtypeStruct((rows // TILE, TILE), jnp.float32),
        ),
        in_specs=[SMEM, SMEM] + [VMEM] * len(operands),
        out_specs=(VMEM, VMEM),
        scratch_shapes=[
            pltpu.VMEM((2 * SIDE * SIDE, rows, TILE), jnp.bfloat16),
            pltpu.VMEM((SIDE * SIDE,) + right_vals.shape, jnp.bfloat16),
        ],
        compiler_params=pltpu.CompilerParams(vmem_limit_bytes=52 * MIB),
    )(at, result_keep, *operands)
    totals = totals.reshape(rows)
    for axis in ("core", "y", "zh"):
        totals = lax.psum(totals, axis)
    width = cols * lax.axis_size("zh") * lax.axis_size("y") * lax.axis_size("core")
    return width * pruned / (totals[:, None] + 1e-06)


def solution(mesh):
    fine = Mesh(mesh.devices.reshape(SIDE, SIDE, SIDE, SIDE, 2), AXES)
    spec = P(("x", "zl"), ("zh", "y", "core"))
    return jax.shard_map(
        per_device,
        mesh=fine,
        in_specs=(spec,) * 7,
        out_specs=spec,
        check_vma=False,
    )
```

time: 404 us -> 181 us (0.45)
  the two profiles are of different devices: /device:TPU:1 before, /device:TPU:8 now
where the time goes in v2:
time: 181 us; the launch traced here: 180 us
  starting transfers between devices  70.7 us (39%)
  waiting for transfers between devices  56.6 us (31%)
  blocking collectives  30.2 us (17%)
  Pallas kernels  14.4 us (8%)
  local copies, waits for them, and re-layouts  4.29 us (2%)
  other arithmetic  3.41 us (2%)
    ppermute x18, starting transfers between devices, step(): return lax.ppermute(value, (axis, 'core'), pairs)  66.7 us
    ppermute x18, waiting for transfers between devices, step(): return lax.ppermute(value, (axis, 'core'), pairs)  56.6 us
    psum x3, blocking collectives, per_device(): totals = lax.psum(totals, axis)  30.2 us
    pallas_call x1, Pallas kernels, per_device(): pl.pallas_call(functools.partial(multiply, [p for _, p in lefts], [p for...  12 us
    unnamed x22, local copies, waits for them, and re-layouts  4.21 us
    ppermute x2, starting transfers between devices, swap(): return lax.ppermute(value, 'core', [(0, 1), (1, 0)])  3.97 us
  transfers between devices with their start and end apart: 20, of which 10 were waited for; matrix products, arithmetic and copies ran while one was open for 0% of the time, Pallas kernels for 0%

profile of v2, /device:TPU:8, one launch (start us, length us, event | category | flops | bytes accessed | tf_op | source)
XLA Modules:
  0.0 180.0 jit_solution(1229185525912540385)
XLA Ops:
  0.0 2.1 %shard_map.73 = (bf16[256,768]{1,0:T(8,128)(2,1)}, bf16[768,128]{1,0:T(8,128)(2,1)}) custom-call(f32[2,6]{1,0:T(2,128)} %refs_0_.1, s32[2,6]{1,0:T(2,128)} %refs_1_.1, bf16[256,768]{1,0:T(8,128)(2,1)} %refs_2_.1, f32[1,6]{1,0:T(1,128)} %bitcast.15, s32[1,6]{1,0:T(1,128)} %bitcast.16, bf16[768,128]{1,0:T(8,128)(2,1)} %refs_5_.1), custom_call_target="tpu_custom_call" | custom-call | tf_op jit(solution)/shard_map/pallas_call | solution.py:68
  2.1 3.8 %collective-permute-start.11 = (bf16[1,256,768]{2,1,0:T(8,128)(2,1)}, bf16[1,256,768]{2,1,0:T(8,128)(2,1)S(1)}, u32[]{:S(2)}, u32[]{:S(2)}) collective-permute-start(bf16[1,256,768]{2,1,0:T(8,128)(2,1)} %bitcast.10), channel_id=1, source_target_pairs={{0,32},{1,97},{32,64},{33,1},{64,96},{65,33},{96,0},{97,65},{2,34}... | collective-permute-start | bytes 1179656 | tf_op jit(solution)/shard_map/ppermute | solution.py:24
  5.9 9.1 %collective-permute-start = (bf16[1,768,128]{2,1,0:T(8,128)(2,1)}, bf16[1,768,128]{2,1,0:T(8,128)(2,1)S(1)}, u32[]{:S(2)}, u32[]{:S(2)}) collective-permute-start(bf16[1,768,128]{2,1,0:T(8,128)(2,1)} %bitcast.12), channel_id=1, source_target_pairs={{0,8},{1,25},{8,16},{9,1},{16,24},{17,9},{24,0},{25,17},{2,10},{3,... | collective-permute-start | bytes 589832 | tf_op jit(solution)/shard_map/ppermute | solution.py:24
  15.0 15.2 %collective-permute-done.refs_1_ = bf16[1,768,128]{2,1,0:T(8,128)(2,1)S(1)} collective-permute-done((bf16[1,768,128]{2,1,0:T(8,128)(2,1)}, bf16[1,768,128]{2,1,0:T(8,128)(2,1)S(1)}, u32[]{:S(2)}, u32[]{:S(2)}) %collective-permute-start) | collective-permute-done | bytes 196640 | tf_op jit(solution)/shard_map/ppermute | solution.py:24
  30.2 3.1 %collective-permute-start.5 = (bf16[1,768,128]{2,1,0:T(8,128)(2,1)S(1)}, bf16[1,768,128]{2,1,0:T(8,128)(2,1)S(1)}, u32[]{:S(2)}, u32[]{:S(2)}) collective-permute-start(bf16[1,768,128]{2,1,0:T(8,128)(2,1)S(1)} %collective-permute-done.refs_1_), channel_id=1, source_target_pairs={{0,8},{1,25},{8,16},{9,1},{16,24},{17,9},{24,0},{25,17},{2,10},{3,... | collective-permute-start | bytes 589832 | tf_op jit(solution)/shard_map/ppermute | solution.py:24
  33.3 0.0 collective-permute-done.11.refs_1_
  33.3 4.4 %collective-permute-start.15 = (bf16[1,256,768]{2,1,0:T(8,128)(2,1)S(1)}, bf16[1,256,768]{2,1,0:T(8,128)(2,1)S(1)}, u32[]{:S(2)}, u32[]{:S(2)}) collective-permute-start(bf16[1,256,768]{2,1,0:T(8,128)(2,1)S(1)} %collective-permute-done.11.refs_1_), channel_id=1, source_target_pairs={{0,32},{1,97},{32,64},{33,1},{64,96},{65,33},{96,0},{97,65},{2,34}... | collective-permute-start | bytes 1179656 | tf_op jit(solution)/shard_map/ppermute | solution.py:24
  37.7 5.1 %collective-permute-done.5.refs_0_ = bf16[1,768,128]{2,1,0:T(8,128)(2,1)S(1)} collective-permute-done((bf16[1,768,128]{2,1,0:T(8,128)(2,1)S(1)}, bf16[1,768,128]{2,1,0:T(8,128)(2,1)S(1)}, u32[]{:S(2)}, u32[]{:S(2)}) %collective-permute-start.5) | collective-permute-done | bytes 196640 | tf_op jit(solution)/shard_map/ppermute | solution.py:24
  42.9 5.3 %collective-permute-start.6 = (bf16[1,768,128]{2,1,0:T(8,128)(2,1)S(1)}, bf16[1,768,128]{2,1,0:T(8,128)(2,1)S(1)}, u32[]{:S(2)}, u32[]{:S(2)}) collective-permute-start(bf16[1,768,128]{2,1,0:T(8,128)(2,1)S(1)} %collective-permute-done.5.refs_0_), channel_id=1, source_target_pairs={{0,8},{1,25},{8,16},{9,1},{16,24},{17,9},{24,0},{25,17},{2,10},{3,... | collective-permute-start | bytes 589832 | tf_op jit(solution)/shard_map/ppermute | solution.py:24
  48.2 0.0 copy-start.8
  48.2 0.9 copy-done.8
  49.2 3.5 %collective-permute-start.1 = (bf16[2,768,128]{2,1,0:T(8,128)(2,1)S(1)}, bf16[2,768,128]{2,1,0:T(8,128)(2,1)S(1)}, u32[]{:S(2)}, u32[]{:S(2)}) collective-permute-start(bf16[2,768,128]{2,1,0:T(8,128)(2,1)S(1)} %shard_map.74.refs_0_), channel_id=1, source_target_pairs={{0,2},{1,7},{2,4},{3,1},{4,6},{5,3},{6,0},{7,5},{8,10},{9,15},{10,... | collective-permute-start | bytes 1179656 | tf_op jit(solution)/shard_map/ppermute | solution.py:24
  52.6 9.4 %collective-permute-done.6.refs_1_ = bf16[1,768,128]{2,1,0:T(8,128)(2,1)S(1)} collective-permute-done((bf16[1,768,128]{2,1,0:T(8,128)(2,1)S(1)}, bf16[1,768,128]{2,1,0:T(8,128)(2,1)S(1)}, u32[]{:S(2)}, u32[]{:S(2)}) %collective-permute-start.6) | collective-permute-done | bytes 196640 | tf_op jit(solution)/shard_map/ppermute | solution.py:24
  62.0 3.5 %collective-permute-start.7 = (bf16[2,768,128]{2,1,0:T(8,128)(2,1)S(1)}, bf16[2,768,128]{2,1,0:T(8,128)(2,1)S(1)}, u32[]{:S(2)}, u32[]{:S(2)}) collective-permute-start(bf16[2,768,128]{2,1,0:T(8,128)(2,1)S(1)} %shard_map.76.refs_0_), channel_id=1, source_target_pairs={{0,2},{1,7},{2,4},{3,1},{4,6},{5,3},{6,0},{7,5},{8,10},{9,15},{10,... | collective-permute-start | bytes 1179656 | tf_op jit(solution)/shard_map/ppermute | solution.py:24
  65.5 0.0 collective-permute-done.15.refs_0_
  65.5 4.4 %collective-permute-start.16 = (bf16[1,256,768]{2,1,0:T(8,128)(2,1)S(1)}, bf16[1,256,768]{2,1,0:T(8,128)(2,1)S(1)}, u32[]{:S(2)}, u32[]{:S(2)}) collective-permute-start(bf16[1,256,768]{2,1,0:T(8,128)(2,1)S(1)} %collective-permute-done.15.refs_0_), channel_id=1, source_target_pairs={{0,32},{1,97},{32,64},{33,1},{64,96},{65,33},{96,0},{97,65},{2,34}... | collective-permute-start | bytes 1179656 | tf_op jit(solution)/shard_map/ppermute | solution.py:24
  69.9 0.0 copy-start.7
  69.9 1.0 copy-done.7
  70.9 0.1 shard_map.78.refs_4_
  71.0 0.0 copy-start.2
  71.0 3.4 %collective-permute-start.12 = (bf16[2,256,768]{2,1,0:T(8,128)(2,1)S(1)}, bf16[2,256,768]{2,1,0:T(8,128)(2,1)S(1)}, u32[]{:S(2)}, u32[]{:S(2)}) collective-permute-start(bf16[2,256,768]{2,1,0:T(8,128)(2,1)S(1)} %shard_map.78.refs_4_), channel_id=1, source_target_pairs={{0,128},{1,385},{128,256},{129,1},{256,384},{257,129},{384,0},{385... | collective-permute-start | bytes 2359304 | tf_op jit(solution)/shard_map/ppermute | solution.py:24
  74.4 0.0 collective-permute-done.1.refs_1_
  74.4 3.2 %collective-permute-start.2 = (bf16[2,768,128]{2,1,0:T(8,128)(2,1)S(1)}, bf16[2,768,128]{2,1,0:T(8,128)(2,1)S(1)}, u32[]{:S(2)}, u32[]{:S(2)}) collective-permute-start(bf16[2,768,128]{2,1,0:T(8,128)(2,1)S(1)} %collective-permute-done.1.refs_1_), channel_id=1, source_target_pairs={{0,2},{1,7},{2,4},{3,1},{4,6},{5,3},{6,0},{7,5},{8,10},{9,15},{10,... | collective-permute-start | bytes 1179656 | tf_op jit(solution)/shard_map/ppermute | solution.py:24
  77.6 0.0 collective-permute-done.7.refs_1_
  77.6 2.1 %collective-permute-start.8 = (bf16[2,768,128]{2,1,0:T(8,128)(2,1)S(1)}, bf16[2,768,128]{2,1,0:T(8,128)(2,1)S(1)}, u32[]{:S(2)}, u32[]{:S(2)}) collective-permute-start(bf16[2,768,128]{2,1,0:T(8,128)(2,1)S(1)} %collective-permute-done.7.refs_1_), channel_id=1, source_target_pairs={{0,2},{1,7},{2,4},{3,1},{4,6},{5,3},{6,0},{7,5},{8,10},{9,15},{10,... | collective-permute-start | bytes 1179656 | tf_op jit(solution)/shard_map/ppermute | solution.py:24
  79.7 0.0 collective-permute-done.16.refs_1_
  79.8 0.1 shard_map.79.refs_8_
  79.8 0.0 copy-start.4
  79.8 3.4 %collective-permute-start.17 = (bf16[2,256,768]{2,1,0:T(8,128)(2,1)S(1)}, bf16[2,256,768]{2,1,0:T(8,128)(2,1)S(1)}, u32[]{:S(2)}, u32[]{:S(2)}) collective-permute-start(bf16[2,256,768]{2,1,0:T(8,128)(2,1)S(1)} %shard_map.79.refs_8_), channel_id=1, source_target_pairs={{0,128},{1,385},{128,256},{129,1},{256,384},{257,129},{384,0},{385... | collective-permute-start | bytes 2359304 | tf_op jit(solution)/shard_map/ppermute | solution.py:24
  83.2 0.8 collective-permute-done.2.refs_2_
  84.1 3.2 %collective-permute-start.3 = (bf16[2,768,128]{2,1,0:T(8,128)(2,1)S(1)}, bf16[2,768,128]{2,1,0:T(8,128)(2,1)S(1)}, u32[]{:S(2)}, u32[]{:S(2)}) collective-permute-start(bf16[2,768,128]{2,1,0:T(8,128)(2,1)S(1)} %collective-permute-done.2.refs_2_), channel_id=1, source_target_pairs={{0,2},{1,7},{2,4},{3,1},{4,6},{5,3},{6,0},{7,5},{8,10},{9,15},{10,... | collective-permute-start | bytes 1179656 | tf_op jit(solution)/shard_map/ppermute | solution.py:24
  87.3 1.0 collective-permute-done.8.refs_2_
  88.3 3.2 %collective-permute-start.9 = (bf16[2,768,128]{2,1,0:T(8,128)(2,1)S(1)}, bf16[2,768,128]{2,1,0:T(8,128)(2,1)S(1)}, u32[]{:S(2)}, u32[]{:S(2)}) collective-permute-start(bf16[2,768,128]{2,1,0:T(8,128)(2,1)S(1)} %collective-permute-done.8.refs_2_), channel_id=1, source_target_pairs={{0,2},{1,7},{2,4},{3,1},{4,6},{5,3},{6,0},{7,5},{8,10},{9,15},{10,... | collective-permute-start | bytes 1179656 | tf_op jit(solution)/shard_map/ppermute | solution.py:24
  91.5 0.0 collective-permute-done.12.refs_5_
  91.5 0.0 copy-start.5
  91.5 3.4 %collective-permute-start.13 = (bf16[2,256,768]{2,1,0:T(8,128)(2,1)S(1)}, bf16[2,256,768]{2,1,0:T(8,128)(2,1)}, u32[]{:S(2)}, u32[]{:S(2)}) collective-permute-start(bf16[2,256,768]{2,1,0:T(8,128)(2,1)S(1)} %collective-permute-done.12.refs_5_), channel_id=1, source_target_pairs={{0,128},{1,385},{128,256},{129,1},{256,384},{257,129},{384,0},{385... | collective-permute-start | bytes 2359304 | tf_op jit(solution)/shard_map/ppermute | solution.py:24
  94.9 0.0 collective-permute-done.3.refs_3_
  94.9 0.1 shard_map.75.refs_0_
  95.0 0.0 copy-start
  95.0 0.0 copy-start.9
  95.0 2.1 %collective-permute-start.4 = (bf16[8,768,128]{2,1,0:T(8,128)(2,1)S(1)}, bf16[8,768,128]{2,1,0:T(8,128)(2,1)}, u32[]{:S(2)}, u32[]{:S(2)}) collective-permute-start(bf16[8,768,128]{2,1,0:T(8,128)(2,1)S(1)} %shard_map.75.refs_0_), channel_id=1, source_target_pairs={{0,1},{1,0},{2,3},{3,2},{4,5},{5,4},{6,7},{7,6},{8,9},{9,8},{10,11... | collective-permute-start | bytes 4718600 | tf_op jit(solution)/shard_map/ppermute | solution.py:28
  97.1 0.8 collective-permute-done.9.refs_3_
  97.9 0.1 shard_map.77.refs_2_
  98.1 1.9 %collective-permute-start.10 = (bf16[8,768,128]{2,1,0:T(8,128)(2,1)S(1)}, bf16[8,768,128]{2,1,0:T(8,128)(2,1)}, u32[]{:S(2)}, u32[]{:S(2)}) collective-permute-start(bf16[8,768,128]{2,1,0:T(8,128)(2,1)S(1)} %shard_map.77.refs_2_), channel_id=1, source_target_pairs={{0,1},{1,0},{2,3},{3,2},{4,5},{5,4},{6,7},{7,6},{8,9},{9,8},{10,11... | collective-permute-start | bytes 4718600 | tf_op jit(solution)/shard_map/ppermute | solution.py:28
  100.0 0.0 collective-permute-done.17.refs_9_
  100.0 3.4 %collective-permute-start.18 = (bf16[2,256,768]{2,1,0:T(8,128)(2,1)S(1)}, bf16[2,256,768]{2,1,0:T(8,128)(2,1)}, u32[]{:S(2)}, u32[]{:S(2)}) collective-permute-start(bf16[2,256,768]{2,1,0:T(8,128)(2,1)S(1)} %collective-permute-done.17.refs_9_), channel_id=1, source_target_pairs={{0,128},{1,385},{128,256},{129,1},{256,384},{257,129},{384,0},{385... | collective-permute-start | bytes 2359304 | tf_op jit(solution)/shard_map/ppermute | solution.py:24
  103.4 3.2 %collective-permute-done.13.refs_6_ = bf16[2,256,768]{2,1,0:T(8,128)(2,1)} collective-permute-done((bf16[2,256,768]{2,1,0:T(8,128)(2,1)S(1)}, bf16[2,256,768]{2,1,0:T(8,128)(2,1)}, u32[]{:S(2)}, u32[]{:S(2)}) %collective-permute-start.13) | collective-permute-done | bytes 786464 | tf_op jit(solution)/shard_map/ppermute | solution.py:24
  106.7 2.2 %collective-permute-start.14 = (bf16[2,256,768]{2,1,0:T(8,128)(2,1)}, bf16[2,256,768]{2,1,0:T(8,128)(2,1)}, u32[]{:S(2)}, u32[]{:S(2)}) collective-permute-start(bf16[2,256,768]{2,1,0:T(8,128)(2,1)} %collective-permute-done.13.refs_6_), channel_id=1, source_target_pairs={{0,128},{1,385},{128,256},{129,1},{256,384},{257,129},{384,0},{385... | collective-permute-start | bytes 2359304 | tf_op jit(solution)/shard_map/ppermute | solution.py:24
  108.9 6.4 %collective-permute-done.18.refs_10_ = bf16[2,256,768]{2,1,0:T(8,128)(2,1)} collective-permute-done((bf16[2,256,768]{2,1,0:T(8,128)(2,1)S(1)}, bf16[2,256,768]{2,1,0:T(8,128)(2,1)}, u32[]{:S(2)}, u32[]{:S(2)}) %collective-permute-start.18) | collective-permute-done | bytes 786464 | tf_op jit(solution)/shard_map/ppermute | solution.py:24
  115.2 2.2 %collective-permute-start.19 = (bf16[2,256,768]{2,1,0:T(8,128)(2,1)}, bf16[2,256,768]{2,1,0:T(8,128)(2,1)}, u32[]{:S(2)}, u32[]{:S(2)}) collective-permute-start(bf16[2,256,768]{2,1,0:T(8,128)(2,1)} %collective-permute-done.18.refs_10_), channel_id=1, source_target_pairs={{0,128},{1,385},{128,256},{129,1},{256,384},{257,129},{384,0},{385... | collective-permute-start | bytes 2359304 | tf_op jit(solution)/shard_map/ppermute | solution.py:24
  117.4 0.1 stack.23.at_ref
  117.5 6.1 %collective-permute-done.14.refs_7_ = bf16[2,256,768]{2,1,0:T(8,128)(2,1)} collective-permute-done((bf16[2,256,768]{2,1,0:T(8,128)(2,1)}, bf16[2,256,768]{2,1,0:T(8,128)(2,1)}, u32[]{:S(2)}, u32[]{:S(2)}) %collective-permute-start.14) | collective-permute-done | bytes 786464 | tf_op jit(solution)/shard_map/ppermute | solution.py:24
  123.7 0.0 collective-permute-done.4.refs_1_
  123.7 0.0 collective-permute-done.10.refs_3_
  123.7 8.4 %collective-permute-done.19.refs_11_ = bf16[2,256,768]{2,1,0:T(8,128)(2,1)} collective-permute-done((bf16[2,256,768]{2,1,0:T(8,128)(2,1)}, bf16[2,256,768]{2,1,0:T(8,128)(2,1)}, u32[]{:S(2)}, u32[]{:S(2)}) %collective-permute-start.19) | collective-permute-done | bytes 786464 | tf_op jit(solution)/shard_map/ppermute | solution.py:24
  132.1 0.0 copy-done.9
  132.1 0.0 copy-start.3
  132.1 1.1 copy-done.3
  133.2 1.1 copy-done.6
  134.4 12.0 %shard_map.80 = (f32[768,768]{1,0:T(8,128)}, f32[6,128]{1,0:T(8,128)S(1)}) custom-call(s32[5]{0:T(128)S(1)} %stack.23.at_ref, s32[6,6]{1,0:T(8,128)S(1)} %copy-done.9, bf16[8,768,128]{2,1,0:T(8,128)(2,1)} %copy-done, bf16[8,768,128]{2,1,0:T(8,128)(2,1)} %collective-permute-done.4.refs_1_, bf16[8,768,128]{2,1,0:T(8,128)(2,1)} %copy-done.1, ...), custom_call_target="tpu_custom_call" | custom-call | tf_op jit(solution)/shard_map/pallas_call | solution.py:144
  146.4 2.4 %psum.21 = f32[768]{0:T(1024)S(1)} all-reduce(f32[768]{0:T(1024)S(1)} %bitcast.14), channel_id=1, replica_groups=mesh['x'=4,'zl'=4,'zh'=4,'y'=4,'core'=2] {'core'}, use_global_device_ids=true, to_apply=%region_0.0 | all-reduce | flops 768 | bytes 6144 | tf_op jit(solution)/shard_map/psum | solution.py:160
  148.8 10.6 %psum.22 = f32[768]{0:T(1024)S(1)} all-reduce(f32[768]{0:T(1024)S(1)} %psum.21), channel_id=1, replica_groups=mesh['x'=4,'zl'=4,'zh'=4,'y'=4,'core'=2] {'y'}, use_global_device_ids=true, to_apply=%region_1.0 | all-reduce | flops 768 | bytes 6144 | tf_op jit(solution)/shard_map/psum | solution.py:160
  159.4 17.2 %psum.23 = f32[768]{0:T(1024)S(1)} all-reduce(f32[768]{0:T(1024)S(1)} %psum.22), channel_id=1, replica_groups=mesh['x'=4,'zl'=4,'zh'=4,'y'=4,'core'=2] {'zh'}, use_global_device_ids=true, to_apply=%region_2.0 | all-reduce | flops 768 | bytes 6144 | tf_op jit(solution)/shard_map/psum | solution.py:160
  176.6 3.4 %multiply_divide_fusion = f32[768,768]{1,0:T(8,128)} fusion(f32[768,768]{1,0:T(8,128)} %get-tuple-element.11, f32[768]{0:T(1024)S(1)} %broadcast_add_fusion), kind=kLoop, calls=%fused_computation | loop fusion | flops 1179648 | bytes 4721664 | tf_op jit(solution)/shard_map/div | solution.py:162
  (12 shorter events, 0.1 us)
Async XLA Ops:
  2.1 31.2 %collective-permute-start.11 = (bf16[1,256,768]{2,1,0:T(8,128)(2,1)}, bf16[1,256,768]{2,1,0:T(8,128)(2,1)S(1)}, u32[]{:S(2)}, u32[]{:S(2)}) collective-permute-start(bf16[1,256,768]{2,1,0:T(8,128)(2,1)} %bitcast.10), channel_id=1, source_target_pairs={{0,32},{1,97},{32,64},{33,1},{64,96},{65,33},{96,0},{97,65},{2,34}... | collective-permute-start | bytes 1179656 | tf_op jit(solution)/shard_map/ppermute | solution.py:24
  5.9 24.3 %collective-permute-start = (bf16[1,768,128]{2,1,0:T(8,128)(2,1)}, bf16[1,768,128]{2,1,0:T(8,128)(2,1)S(1)}, u32[]{:S(2)}, u32[]{:S(2)}) collective-permute-start(bf16[1,768,128]{2,1,0:T(8,128)(2,1)} %bitcast.12), channel_id=1, source_target_pairs={{0,8},{1,25},{8,16},{9,1},{16,24},{17,9},{24,0},{25,17},{2,10},{3,... | collective-permute-start | bytes 589832 | tf_op jit(solution)/shard_map/ppermute | solution.py:24
  30.2 12.7 %collective-permute-start.5 = (bf16[1,768,128]{2,1,0:T(8,128)(2,1)S(1)}, bf16[1,768,128]{2,1,0:T(8,128)(2,1)S(1)}, u32[]{:S(2)}, u32[]{:S(2)}) collective-permute-start(bf16[1,768,128]{2,1,0:T(8,128)(2,1)S(1)} %collective-permute-done.refs_1_), channel_id=1, source_target_pairs={{0,8},{1,25},{8,16},{9,1},{16,24},{17,9},{24,0},{25,17},{2,10},{3,... | collective-permute-start | bytes 589832 | tf_op jit(solution)/shard_map/ppermute | solution.py:24
  33.3 32.2 %collective-permute-start.15 = (bf16[1,256,768]{2,1,0:T(8,128)(2,1)S(1)}, bf16[1,256,768]{2,1,0:T(8,128)(2,1)S(1)}, u32[]{:S(2)}, u32[]{:S(2)}) collective-permute-start(bf16[1,256,768]{2,1,0:T(8,128)(2,1)S(1)} %collective-permute-done.11.refs_1_), channel_id=1, source_target_pairs={{0,32},{1,97},{32,64},{33,1},{64,96},{65,33},{96,0},{97,65},{2,34}... | collective-permute-start | bytes 1179656 | tf_op jit(solution)/shard_map/ppermute | solution.py:24
  42.9 19.2 %collective-permute-start.6 = (bf16[1,768,128]{2,1,0:T(8,128)(2,1)S(1)}, bf16[1,768,128]{2,1,0:T(8,128)(2,1)S(1)}, u32[]{:S(2)}, u32[]{:S(2)}) collective-permute-start(bf16[1,768,128]{2,1,0:T(8,128)(2,1)S(1)} %collective-permute-done.5.refs_0_), channel_id=1, source_target_pairs={{0,8},{1,25},{8,16},{9,1},{16,24},{17,9},{24,0},{25,17},{2,10},{3,... | collective-permute-start | bytes 589832 | tf_op jit(solution)/shard_map/ppermute | solution.py:24
  48.2 0.9 copy-start.8
  49.2 25.2 %collective-permute-start.1 = (bf16[2,768,128]{2,1,0:T(8,128)(2,1)S(1)}, bf16[2,768,128]{2,1,0:T(8,128)(2,1)S(1)}, u32[]{:S(2)}, u32[]{:S(2)}) collective-permute-start(bf16[2,768,128]{2,1,0:T(8,128)(2,1)S(1)} %shard_map.74.refs_0_), channel_id=1, source_target_pairs={{0,2},{1,7},{2,4},{3,1},{4,6},{5,3},{6,0},{7,5},{8,10},{9,15},{10,... | collective-permute-start | bytes 1179656 | tf_op jit(solution)/shard_map/ppermute | solution.py:24
  62.0 15.6 %collective-permute-start.7 = (bf16[2,768,128]{2,1,0:T(8,128)(2,1)S(1)}, bf16[2,768,128]{2,1,0:T(8,128)(2,1)S(1)}, u32[]{:S(2)}, u32[]{:S(2)}) collective-permute-start(bf16[2,768,128]{2,1,0:T(8,128)(2,1)S(1)} %shard_map.76.refs_0_), channel_id=1, source_target_pairs={{0,2},{1,7},{2,4},{3,1},{4,6},{5,3},{6,0},{7,5},{8,10},{9,15},{10,... | collective-permute-start | bytes 1179656 | tf_op jit(solution)/shard_map/ppermute | solution.py:24
  65.5 14.2 %collective-permute-start.16 = (bf16[1,256,768]{2,1,0:T(8,128)(2,1)S(1)}, bf16[1,256,768]{2,1,0:T(8,128)(2,1)S(1)}, u32[]{:S(2)}, u32[]{:S(2)}) collective-permute-start(bf16[1,256,768]{2,1,0:T(8,128)(2,1)S(1)} %collective-permute-done.15.refs_0_), channel_id=1, source_target_pairs={{0,32},{1,97},{32,64},{33,1},{64,96},{65,33},{96,0},{97,65},{2,34}... | collective-permute-start | bytes 1179656 | tf_op jit(solution)/shard_map/ppermute | solution.py:24
  69.9 1.0 copy-start.7
  71.0 27.1 %copy-start.2 = (bf16[2,256,768]{2,1,0:T(8,128)(2,1)}, bf16[2,256,768]{2,1,0:T(8,128)(2,1)S(1)}, u32[]{:S(2)}) copy-start(bf16[2,256,768]{2,1,0:T(8,128)(2,1)S(1)} %shard_map.78.refs_4_) | copy-start | bytes 2359300
  71.0 20.5 %collective-permute-start.12 = (bf16[2,256,768]{2,1,0:T(8,128)(2,1)S(1)}, bf16[2,256,768]{2,1,0:T(8,128)(2,1)S(1)}, u32[]{:S(2)}, u32[]{:S(2)}) collective-permute-start(bf16[2,256,768]{2,1,0:T(8,128)(2,1)S(1)} %shard_map.78.refs_4_), channel_id=1, source_target_pairs={{0,128},{1,385},{128,256},{129,1},{256,384},{257,129},{384,0},{385... | collective-permute-start | bytes 2359304 | tf_op jit(solution)/shard_map/ppermute | solution.py:24
  74.4 9.7 %collective-permute-start.2 = (bf16[2,768,128]{2,1,0:T(8,128)(2,1)S(1)}, bf16[2,768,128]{2,1,0:T(8,128)(2,1)S(1)}, u32[]{:S(2)}, u32[]{:S(2)}) collective-permute-start(bf16[2,768,128]{2,1,0:T(8,128)(2,1)S(1)} %collective-permute-done.1.refs_1_), channel_id=1, source_target_pairs={{0,2},{1,7},{2,4},{3,1},{4,6},{5,3},{6,0},{7,5},{8,10},{9,15},{10,... | collective-permute-start | bytes 1179656 | tf_op jit(solution)/shard_map/ppermute | solution.py:24
  77.6 10.7 %collective-permute-start.8 = (bf16[2,768,128]{2,1,0:T(8,128)(2,1)S(1)}, bf16[2,768,128]{2,1,0:T(8,128)(2,1)S(1)}, u32[]{:S(2)}, u32[]{:S(2)}) collective-permute-start(bf16[2,768,128]{2,1,0:T(8,128)(2,1)S(1)} %collective-permute-done.7.refs_1_), channel_id=1, source_target_pairs={{0,2},{1,7},{2,4},{3,1},{4,6},{5,3},{6,0},{7,5},{8,10},{9,15},{10,... | collective-permute-start | bytes 1179656 | tf_op jit(solution)/shard_map/ppermute | solution.py:24
  79.8 18.2 %copy-start.4 = (bf16[2,256,768]{2,1,0:T(8,128)(2,1)}, bf16[2,256,768]{2,1,0:T(8,128)(2,1)S(1)}, u32[]{:S(2)}) copy-start(bf16[2,256,768]{2,1,0:T(8,128)(2,1)S(1)} %shard_map.79.refs_8_) | copy-start | bytes 2359300
  79.8 20.2 %collective-permute-start.17 = (bf16[2,256,768]{2,1,0:T(8,128)(2,1)S(1)}, bf16[2,256,768]{2,1,0:T(8,128)(2,1)S(1)}, u32[]{:S(2)}, u32[]{:S(2)}) collective-permute-start(bf16[2,256,768]{2,1,0:T(8,128)(2,1)S(1)} %shard_map.79.refs_8_), channel_id=1, source_target_pairs={{0,128},{1,385},{128,256},{129,1},{256,384},{257,129},{384,0},{385... | collective-permute-start | bytes 2359304 | tf_op jit(solution)/shard_map/ppermute | solution.py:24
  84.1 10.8 %collective-permute-start.3 = (bf16[2,768,128]{2,1,0:T(8,128)(2,1)S(1)}, bf16[2,768,128]{2,1,0:T(8,128)(2,1)S(1)}, u32[]{:S(2)}, u32[]{:S(2)}) collective-permute-start(bf16[2,768,128]{2,1,0:T(8,128)(2,1)S(1)} %collective-permute-done.2.refs_2_), channel_id=1, source_target_pairs={{0,2},{1,7},{2,4},{3,1},{4,6},{5,3},{6,0},{7,5},{8,10},{9,15},{10,... | collective-permute-start | bytes 1179656 | tf_op jit(solution)/shard_map/ppermute | solution.py:24
  88.3 9.7 %collective-permute-start.9 = (bf16[2,768,128]{2,1,0:T(8,128)(2,1)S(1)}, bf16[2,768,128]{2,1,0:T(8,128)(2,1)S(1)}, u32[]{:S(2)}, u32[]{:S(2)}) collective-permute-start(bf16[2,768,128]{2,1,0:T(8,128)(2,1)S(1)} %collective-permute-done.8.refs_2_), channel_id=1, source_target_pairs={{0,2},{1,7},{2,4},{3,1},{4,6},{5,3},{6,0},{7,5},{8,10},{9,15},{10,... | collective-permute-start | bytes 1179656 | tf_op jit(solution)/shard_map/ppermute | solution.py:24
  91.5 6.6 %copy-start.5 = (bf16[2,256,768]{2,1,0:T(8,128)(2,1)}, bf16[2,256,768]{2,1,0:T(8,128)(2,1)S(1)}, u32[]{:S(2)}) copy-start(bf16[2,256,768]{2,1,0:T(8,128)(2,1)S(1)} %collective-permute-done.12.refs_5_) | copy-start | bytes 2359300
  91.5 15.2 %collective-permute-start.13 = (bf16[2,256,768]{2,1,0:T(8,128)(2,1)S(1)}, bf16[2,256,768]{2,1,0:T(8,128)(2,1)}, u32[]{:S(2)}, u32[]{:S(2)}) collective-permute-start(bf16[2,256,768]{2,1,0:T(8,128)(2,1)S(1)} %collective-permute-done.12.refs_5_), channel_id=1, source_target_pairs={{0,128},{1,385},{128,256},{129,1},{256,384},{257,129},{384,0},{385... | collective-permute-start | bytes 2359304 | tf_op jit(solution)/shard_map/ppermute | solution.py:24
  95.0 37.1 %copy-start = (bf16[8,768,128]{2,1,0:T(8,128)(2,1)}, bf16[8,768,128]{2,1,0:T(8,128)(2,1)S(1)}, u32[]{:S(2)}) copy-start(bf16[8,768,128]{2,1,0:T(8,128)(2,1)S(1)} %shard_map.75.refs_0_) | copy-start | bytes 4718596
  95.0 37.1 %copy-start.9 = (s32[6,6]{1,0:T(8,128)S(1)}, s32[6,6]{1,0:T(8,128)}, u32[]{:S(2)}) copy-start(s32[6,6]{1,0:T(8,128)} %keep_ref.1) | copy-start | bytes 436
  95.0 28.6 %collective-permute-start.4 = (bf16[8,768,128]{2,1,0:T(8,128)(2,1)S(1)}, bf16[8,768,128]{2,1,0:T(8,128)(2,1)}, u32[]{:S(2)}, u32[]{:S(2)}) collective-permute-start(bf16[8,768,128]{2,1,0:T(8,128)(2,1)S(1)} %shard_map.75.refs_0_), channel_id=1, source_target_pairs={{0,1},{1,0},{2,3},{3,2},{4,5},{5,4},{6,7},{7,6},{8,9},{9,8},{10,11... | collective-permute-start | bytes 4718600 | tf_op jit(solution)/shard_map/ppermute | solution.py:28
  98.1 34.0 %copy-start.1 = (bf16[8,768,128]{2,1,0:T(8,128)(2,1)}, bf16[8,768,128]{2,1,0:T(8,128)(2,1)S(1)}, u32[]{:S(2)}) copy-start(bf16[8,768,128]{2,1,0:T(8,128)(2,1)S(1)} %shard_map.77.refs_2_) | copy-start | bytes 4718596
  98.1 25.6 %collective-permute-start.10 = (bf16[8,768,128]{2,1,0:T(8,128)(2,1)S(1)}, bf16[8,768,128]{2,1,0:T(8,128)(2,1)}, u32[]{:S(2)}, u32[]{:S(2)}) collective-permute-start(bf16[8,768,128]{2,1,0:T(8,128)(2,1)S(1)} %shard_map.77.refs_2_), channel_id=1, source_target_pairs={{0,1},{1,0},{2,3},{3,2},{4,5},{5,4},{6,7},{7,6},{8,9},{9,8},{10,11... | collective-permute-start | bytes 4718600 | tf_op jit(solution)/shard_map/ppermute | solution.py:28
  100.0 6.7 %copy-start.10 = (bf16[2,256,768]{2,1,0:T(8,128)(2,1)}, bf16[2,256,768]{2,1,0:T(8,128)(2,1)S(1)}, u32[]{:S(2)}) copy-start(bf16[2,256,768]{2,1,0:T(8,128)(2,1)S(1)} %collective-permute-done.17.refs_9_) | copy-start | bytes 2359300
  100.0 15.2 %collective-permute-start.18 = (bf16[2,256,768]{2,1,0:T(8,128)(2,1)S(1)}, bf16[2,256,768]{2,1,0:T(8,128)(2,1)}, u32[]{:S(2)}, u32[]{:S(2)}) collective-permute-start(bf16[2,256,768]{2,1,0:T(8,128)(2,1)S(1)} %collective-permute-done.17.refs_9_), channel_id=1, source_target_pairs={{0,128},{1,385},{128,256},{129,1},{256,384},{257,129},{384,0},{385... | collective-permute-start | bytes 2359304 | tf_op jit(solution)/shard_map/ppermute | solution.py:24
  106.7 17.0 %collective-permute-start.14 = (bf16[2,256,768]{2,1,0:T(8,128)(2,1)}, bf16[2,256,768]{2,1,0:T(8,128)(2,1)}, u32[]{:S(2)}, u32[]{:S(2)}) collective-permute-start(bf16[2,256,768]{2,1,0:T(8,128)(2,1)} %collective-permute-done.13.refs_6_), channel_id=1, source_target_pairs={{0,128},{1,385},{128,256},{129,1},{256,384},{257,129},{384,0},{385... | collective-permute-start | bytes 2359304 | tf_op jit(solution)/shard_map/ppermute | solution.py:24
  115.2 16.9 %collective-permute-start.19 = (bf16[2,256,768]{2,1,0:T(8,128)(2,1)}, bf16[2,256,768]{2,1,0:T(8,128)(2,1)}, u32[]{:S(2)}, u32[]{:S(2)}) collective-permute-start(bf16[2,256,768]{2,1,0:T(8,128)(2,1)} %collective-permute-done.18.refs_10_), channel_id=1, source_target_pairs={{0,128},{1,385},{128,256},{129,1},{256,384},{257,129},{384,0},{385... | collective-permute-start | bytes 2359304 | tf_op jit(solution)/shard_map/ppermute | solution.py:24
  132.1 1.1 copy-start.3
  133.2 1.1 copy-start.6

commit v3 on v2

--- a/solution.py
+++ b/solution.py
@@ -42,7 +42,7 @@
         out_shape=jax.ShapeDtypeStruct(shape, jnp.bfloat16),
         in_specs=[VMEM] * (len(parts) + len(after)),
         out_specs=VMEM,
-        compiler_params=pltpu.CompilerParams(vmem_limit_bytes=8 * MIB),
+        compiler_params=pltpu.CompilerParams(vmem_limit_bytes=10 * MIB),
     )(*parts, *after)
 
 
@@ -75,34 +75,31 @@
     )(*operands)
 
 
-def multiply(left_at, right_at, at_ref, keep_ref, *refs):
-    left_refs, refs = refs[:len(left_at)], refs[len(left_at):]
-    right_refs, refs = refs[:len(right_at)], refs[len(right_at):]
-    pruned_ref, total_ref, left, right = refs
+def multiply(left_at, at_ref, keep_ref, *refs):
+    left_refs, right_refs = refs[:len(left_at)], refs[len(left_at):-3]
+    pruned_ref, total_ref, left = refs[-3:]
     x, zl, zh, y, core = (at_ref[i] for i in range(5))
     way = 1 - 2 * core
 
-    def left_place(first, lanes, first_step, sign, i):
-        k, s = first + lax.rem(i, lanes), first_step + lax.div(i, lanes)
-        block = lax.rem(zh - k * sign * way + SIDE, SIDE) * SIDE + lax.rem(y - s * sign * way + SIDE, SIDE)
-        return block * 2 + (core if sign > 0 else 1 - core)
+    for ref, (first, lanes, sign) in zip(left_refs, left_at):
+        def put(i, carry, ref=ref, first=first, lanes=lanes, sign=sign):
+            k, s = first + lax.rem(i, lanes), lax.div(i, lanes)
+            across = lax.rem((x - zh + k * sign * way) * way + 4 * SIDE, SIDE)
+            along = lax.rem((zl - y + s * sign * way) * way + 4 * SIDE, SIDE)
+            block = lax.div(along, 2) * (2 * SIDE) + across * 2 + lax.rem(along, 2)
+            left[block * 2 + (core if sign > 0 else 1 - core)] = ref[i]
+            return carry
 
-    def right_place(first, lanes, first_step, i):
-        k, s = first + lax.rem(i, lanes), first_step + lax.div(i, lanes)
-        return lax.rem(x - s * way + SIDE, SIDE) * SIDE + lax.rem(zl - k * way + SIDE, SIDE)
-
-    for held, place, places, given in ((left, left_place, left_at, left_refs), (right, right_place, right_at, right_refs)):
-        for ref, at in zip(given, places):
-            def put(i, carry, held=held, place=place, ref=ref, at=at):
-                held[place(*at, i)] = ref[i]
-                return carry
-
-            lax.fori_loop(0, ref.shape[0], put, 0)
-    blocks, rows = left.shape[0], 2 * TILE
-    cols = right.shape[2]
+        lax.fori_loop(0, ref.shape[0], put, 0)
+    rows, depth, cols = 2 * TILE, right_refs[0].shape[1], right_refs[0].shape[2]
     for m in range(left.shape[1] // rows):
-        lhs = jnp.concatenate([left[k, m * rows:(m + 1) * rows, :] for k in range(blocks)], axis=1)
-        product = jnp.dot(lhs, right[...].reshape(blocks * TILE, cols), preferred_element_type=jnp.float32)
+        product, at = None, 0
+        for ref in right_refs:
+            count = ref.shape[0] * depth // TILE
+            lhs = jnp.concatenate([left[k, m * rows:(m + 1) * rows, :] for k in range(at, at + count)], axis=1)
+            part = jnp.dot(lhs, ref[...].reshape(-1, cols), preferred_element_type=jnp.float32)
+            product = part if product is None else product + part
+            at += count
         for r in range(rows // TILE):
             total = jnp.zeros((TILE, TILE), jnp.float32)
             i = m * (rows // TILE) + r
@@ -112,6 +109,21 @@
                 pruned_ref[i * TILE:(i + 1) * TILE, n * TILE:(n + 1) * TILE] = block
                 total = total + block
             total_ref[i:i + 1, :] = jnp.sum(total.T, axis=0, keepdims=True)
+
+
+def normalize(width, pruned_ref, shares_ref, flow_ref, held, sem):
+    factors = width / (jnp.sum(shares_ref[...], axis=0, keepdims=True) + 1e-06)
+    copies = []
+    for i in range(held.shape[0] // TILE):
+        at = slice(i * TILE, (i + 1) * TILE)
+        factor = jnp.broadcast_to(factors[:, at], (TILE, TILE)).T
+        for n in range(held.shape[1] // TILE):
+            to = (at, slice(n * TILE, (n + 1) * TILE))
+            held[to] = pruned_ref[to] * factor
+        copies.append(pltpu.make_async_copy(held.at[pl.ds(i * TILE, TILE)], flow_ref.at[pl.ds(i * TILE, TILE)], sem))
+        copies[-1].start()
+    for copy in copies:
+        copy.wait()
 
 
 def per_device(left_vals, left_scale, left_keep, right_vals, right_scale, right_keep, result_keep):
@@ -132,17 +144,16 @@
         for _ in range(SIDE - 1):
             own.append(step(own[-1], "y"))
         own = join(own)
-        lefts.append((own, (first, 2, 0, 1)))
-        lefts.append((swap(own), (first, 2, 0, -1)))
+        lefts.append((own, (first, 2, 1)))
+        lefts.append((swap(own), (first, 2, -1)))
     for first in (0, 2):
-        block = join(lane[first:first + 2])
-        rights.append((block, (first, 2, 0)))
-        for s in range(1, SIDE):
-            block = step(block, "x")
-            rights.append((block, (first, 2, s)))
-    operands = [v for v, _ in lefts + rights]
+        blocks = [join(lane[first:first + 2])]
+        for _ in range(SIDE - 1):
+            blocks.append(step(blocks[-1], "x"))
+        rights += blocks if first else [join(blocks)]
+    operands = [v for v, _ in lefts] + rights
     pruned, totals = pl.pallas_call(
-        functools.partial(multiply, [p for _, p in lefts], [p for _, p in rights]),
+        functools.partial(multiply, [p for _, p in lefts]),
         out_shape=(
             jax.ShapeDtypeStruct((rows, cols), jnp.float32),
             jax.ShapeDtypeStruct((rows // TILE, TILE), jnp.float32),
@@ -151,15 +162,22 @@
         out_specs=(VMEM, VMEM),
         scratch_shapes=[
             pltpu.VMEM((2 * SIDE * SIDE, rows, TILE), jnp.bfloat16),
-            pltpu.VMEM((SIDE * SIDE,) + right_vals.shape, jnp.bfloat16),
         ],
-        compiler_params=pltpu.CompilerParams(vmem_limit_bytes=52 * MIB),
+        compiler_params=pltpu.CompilerParams(vmem_limit_bytes=20 * MIB),
     )(at, result_keep, *operands)
     totals = totals.reshape(rows)
-    for axis in ("core", "y", "zh"):
-        totals = lax.psum(totals, axis)
+    totals = lax.psum(totals, "core")
+    spread = jnp.broadcast_to(totals, (SIDE * SIDE, rows))
+    shares = lax.all_to_all(spread, ("zh", "y"), 0, 0)
     width = cols * lax.axis_size("zh") * lax.axis_size("y") * lax.axis_size("core")
-    return width * pruned / (totals[:, None] + 1e-06)
+    return pl.pallas_call(
+        functools.partial(normalize, float(width)),
+        out_shape=jax.ShapeDtypeStruct((rows, cols), jnp.float32),
+        in_specs=[VMEM, VMEM],
+        out_specs=ANY,
+        scratch_shapes=[pltpu.VMEM((rows, cols), jnp.float32), pltpu.SemaphoreType.DMA],
+        compiler_params=pltpu.CompilerParams(vmem_limit_bytes=8 * MIB),
+    )(pruned, shares)
 
 
 def solution(mesh):

time: 181 us -> 174 us (0.961)
  the two profiles are of different devices: /device:TPU:8 before, /device:TPU:1 now
where the time goes in v3:
time: 174 us; the launch traced here: 173 us
  starting transfers between devices  102 us (59%)
  blocking collectives  26.7 us (15%)
  waiting for transfers between devices  22 us (13%)
  Pallas kernels  14.1 us (8%)
  local copies, waits for them, and re-layouts  7.3 us (4%)
    ppermute x18, starting transfers between devices, step(): return lax.ppermute(value, (axis, 'core'), pairs)  92.4 us
    all_to_all x1, blocking collectives, per_device(): shares = lax.all_to_all(spread, ('zh', 'y'), 0, 0)  22.5 us
    ppermute x18, waiting for transfers between devices, step(): return lax.ppermute(value, (axis, 'core'), pairs)  22 us
    ppermute x2, starting transfers between devices, swap(): return lax.ppermute(value, 'core', [(0, 1), (1, 0)])  9.89 us
    pallas_call x1, Pallas kernels, per_device(): pl.pallas_call(functools.partial(multiply, [p for _, p in lefts]), out_sh...  8.49 us
    unnamed x27, local copies, waits for them, and re-layouts  7.18 us
    psum x1, blocking collectives, per_device(): totals = lax.psum(totals, 'core')  4.18 us
  transfers between devices with their start and end apart: 20, of which 6 were waited for; matrix products, arithmetic and copies ran while one was open for 0% of the time, Pallas kernels for 1%

profile of v3, /device:TPU:1, one launch (start us, length us, event | category | flops | bytes accessed | tf_op | source)
XLA Modules:
  0.0 172.9 jit_solution(3922014048029782559)
XLA Ops:
  0.0 2.1 %shard_map.73 = (bf16[256,768]{1,0:T(8,128)(2,1)}, bf16[768,128]{1,0:T(8,128)(2,1)}) custom-call(f32[2,6]{1,0:T(2,128)} %refs_0_.1, s32[2,6]{1,0:T(2,128)} %refs_1_.1, bf16[256,768]{1,0:T(8,128)(2,1)} %refs_2_.1, f32[1,6]{1,0:T(1,128)} %bitcast.19, s32[1,6]{1,0:T(1,128)} %bitcast.20, bf16[768,128]{1,0:T(8,128)(2,1)} %refs_5_.1), custom_call_target="tpu_custom_call" | custom-call | tf_op jit(solution)/shard_map/pallas_call | solution.py:68
  2.1 0.0 copy-start.10
  2.1 7.2 %collective-permute-start.11 = (bf16[1,256,768]{2,1,0:T(8,128)(2,1)}, bf16[1,256,768]{2,1,0:T(8,128)(2,1)S(1)}, u32[]{:S(2)}, u32[]{:S(2)}) collective-permute-start(bf16[1,256,768]{2,1,0:T(8,128)(2,1)} %bitcast.13), channel_id=1, source_target_pairs={{0,32},{1,97},{32,64},{33,1},{64,96},{65,33},{96,0},{97,65},{2,34}... | collective-permute-start | bytes 1179656 | tf_op jit(solution)/shard_map/ppermute | solution.py:24
  9.3 9.8 %collective-permute-start = (bf16[1,768,128]{2,1,0:T(8,128)(2,1)}, bf16[1,768,128]{2,1,0:T(8,128)(2,1)S(1)}, u32[]{:S(2)}, u32[]{:S(2)}) collective-permute-start(bf16[1,768,128]{2,1,0:T(8,128)(2,1)} %bitcast.16), channel_id=1, source_target_pairs={{0,8},{1,25},{8,16},{9,1},{16,24},{17,9},{24,0},{25,17},{2,10},{3,... | collective-permute-start | bytes 589832 | tf_op jit(solution)/shard_map/ppermute | solution.py:24
  19.1 5.4 %collective-permute-done.refs_1_ = bf16[1,768,128]{2,1,0:T(8,128)(2,1)S(1)} collective-permute-done((bf16[1,768,128]{2,1,0:T(8,128)(2,1)}, bf16[1,768,128]{2,1,0:T(8,128)(2,1)S(1)}, u32[]{:S(2)}, u32[]{:S(2)}) %collective-permute-start) | collective-permute-done | bytes 196640 | tf_op jit(solution)/shard_map/ppermute | solution.py:24
  24.5 7.8 %collective-permute-start.5 = (bf16[1,768,128]{2,1,0:T(8,128)(2,1)S(1)}, bf16[1,768,128]{2,1,0:T(8,128)(2,1)S(1)}, u32[]{:S(2)}, u32[]{:S(2)}) collective-permute-start(bf16[1,768,128]{2,1,0:T(8,128)(2,1)S(1)} %collective-permute-done.refs_1_), channel_id=1, source_target_pairs={{0,8},{1,25},{8,16},{9,1},{16,24},{17,9},{24,0},{25,17},{2,10},{3,... | collective-permute-start | bytes 589832 | tf_op jit(solution)/shard_map/ppermute | solution.py:24
  32.2 0.0 collective-permute-done.11.refs_1_
  32.2 7.2 %collective-permute-start.15 = (bf16[1,256,768]{2,1,0:T(8,128)(2,1)S(1)}, bf16[1,256,768]{2,1,0:T(8,128)(2,1)S(1)}, u32[]{:S(2)}, u32[]{:S(2)}) collective-permute-start(bf16[1,256,768]{2,1,0:T(8,128)(2,1)S(1)} %collective-permute-done.11.refs_1_), channel_id=1, source_target_pairs={{0,32},{1,97},{32,64},{33,1},{64,96},{65,33},{96,0},{97,65},{2,34}... | collective-permute-start | bytes 1179656 | tf_op jit(solution)/shard_map/ppermute | solution.py:24
  39.4 0.0 collective-permute-done.5.refs_0_
  39.4 7.6 %collective-permute-start.6 = (bf16[1,768,128]{2,1,0:T(8,128)(2,1)S(1)}, bf16[1,768,128]{2,1,0:T(8,128)(2,1)S(1)}, u32[]{:S(2)}, u32[]{:S(2)}) collective-permute-start(bf16[1,768,128]{2,1,0:T(8,128)(2,1)S(1)} %collective-permute-done.5.refs_0_), channel_id=1, source_target_pairs={{0,8},{1,25},{8,16},{9,1},{16,24},{17,9},{24,0},{25,17},{2,10},{3,... | collective-permute-start | bytes 589832 | tf_op jit(solution)/shard_map/ppermute | solution.py:24
  47.0 0.9 copy-done.11
  48.0 8.7 %collective-permute-start.1 = (bf16[2,768,128]{2,1,0:T(8,128)(2,1)S(1)}, bf16[2,768,128]{2,1,0:T(8,128)(2,1)S(1)}, u32[]{:S(2)}, u32[]{:S(2)}) collective-permute-start(bf16[2,768,128]{2,1,0:T(8,128)(2,1)S(1)} %shard_map.74.refs_0_), channel_id=1, source_target_pairs={{0,2},{1,7},{2,4},{3,1},{4,6},{5,3},{6,0},{7,5},{8,10},{9,15},{10,... | collective-permute-start | bytes 1179656 | tf_op jit(solution)/shard_map/ppermute | solution.py:24
  56.6 0.0 collective-permute-done.6.refs_1_
  56.7 2.4 %collective-permute-start.7 = (bf16[2,768,128]{2,1,0:T(8,128)(2,1)S(1)}, bf16[2,768,128]{2,1,0:T(8,128)(2,1)S(1)}, u32[]{:S(2)}, u32[]{:S(2)}) collective-permute-start(bf16[2,768,128]{2,1,0:T(8,128)(2,1)S(1)} %shard_map.76.refs_0_), channel_id=1, source_target_pairs={{0,2},{1,7},{2,4},{3,1},{4,6},{5,3},{6,0},{7,5},{8,10},{9,15},{10,... | collective-permute-start | bytes 1179656 | tf_op jit(solution)/shard_map/ppermute | solution.py:24
  59.1 0.0 collective-permute-done.15.refs_0_
  59.1 9.8 %collective-permute-start.16 = (bf16[1,256,768]{2,1,0:T(8,128)(2,1)S(1)}, bf16[1,256,768]{2,1,0:T(8,128)(2,1)S(1)}, u32[]{:S(2)}, u32[]{:S(2)}) collective-permute-start(bf16[1,256,768]{2,1,0:T(8,128)(2,1)S(1)} %collective-permute-done.15.refs_0_), channel_id=1, source_target_pairs={{0,32},{1,97},{32,64},{33,1},{64,96},{65,33},{96,0},{97,65},{2,34}... | collective-permute-start | bytes 1179656 | tf_op jit(solution)/shard_map/ppermute | solution.py:24
  68.9 0.1 shard_map.78.refs_0_
  69.0 0.0 copy-start
  69.0 4.4 %collective-permute-start.12 = (bf16[2,256,768]{2,1,0:T(8,128)(2,1)S(1)}, bf16[2,256,768]{2,1,0:T(8,128)(2,1)S(1)}, u32[]{:S(2)}, u32[]{:S(2)}) collective-permute-start(bf16[2,256,768]{2,1,0:T(8,128)(2,1)S(1)} %shard_map.78.refs_0_), channel_id=1, source_target_pairs={{0,128},{1,385},{128,256},{129,1},{256,384},{257,129},{384,0},{385... | collective-permute-start | bytes 2359304 | tf_op jit(solution)/shard_map/ppermute | solution.py:24
  73.4 0.0 collective-permute-done.1.refs_1_
  73.4 2.4 %collective-permute-start.2 = (bf16[2,768,128]{2,1,0:T(8,128)(2,1)S(1)}, bf16[2,768,128]{2,1,0:T(8,128)(2,1)S(1)}, u32[]{:S(2)}, u32[]{:S(2)}) collective-permute-start(bf16[2,768,128]{2,1,0:T(8,128)(2,1)S(1)} %collective-permute-done.1.refs_1_), channel_id=1, source_target_pairs={{0,2},{1,7},{2,4},{3,1},{4,6},{5,3},{6,0},{7,5},{8,10},{9,15},{10,... | collective-permute-start | bytes 1179656 | tf_op jit(solution)/shard_map/ppermute | solution.py:24
  75.8 0.0 collective-permute-done.7.refs_1_
  75.8 2.1 %collective-permute-start.8 = (bf16[2,768,128]{2,1,0:T(8,128)(2,1)S(1)}, bf16[2,768,128]{2,1,0:T(8,128)(2,1)S(1)}, u32[]{:S(2)}, u32[]{:S(2)}) collective-permute-start(bf16[2,768,128]{2,1,0:T(8,128)(2,1)S(1)} %collective-permute-done.7.refs_1_), channel_id=1, source_target_pairs={{0,2},{1,7},{2,4},{3,1},{4,6},{5,3},{6,0},{7,5},{8,10},{9,15},{10,... | collective-permute-start | bytes 1179656 | tf_op jit(solution)/shard_map/ppermute | solution.py:24
  77.9 1.7 %collective-permute-done.16.refs_1_ = bf16[1,256,768]{2,1,0:T(8,128)(2,1)S(1)} collective-permute-done((bf16[1,256,768]{2,1,0:T(8,128)(2,1)S(1)}, bf16[1,256,768]{2,1,0:T(8,128)(2,1)S(1)}, u32[]{:S(2)}, u32[]{:S(2)}) %collective-permute-start.16) | collective-permute-done | bytes 393248 | tf_op jit(solution)/shard_map/ppermute | solution.py:24
  79.6 0.1 shard_map.80.refs_5_
  79.7 0.0 copy-start.2
  79.7 4.4 %collective-permute-start.17 = (bf16[2,256,768]{2,1,0:T(8,128)(2,1)S(1)}, bf16[2,256,768]{2,1,0:T(8,128)(2,1)S(1)}, u32[]{:S(2)}, u32[]{:S(2)}) collective-permute-start(bf16[2,256,768]{2,1,0:T(8,128)(2,1)S(1)} %shard_map.80.refs_5_), channel_id=1, source_target_pairs={{0,128},{1,385},{128,256},{129,1},{256,384},{257,129},{384,0},{385... | collective-permute-start | bytes 2359304 | tf_op jit(solution)/shard_map/ppermute | solution.py:24
  84.1 0.0 collective-permute-done.2.refs_2_
  84.1 2.4 %collective-permute-start.3 = (bf16[2,768,128]{2,1,0:T(8,128)(2,1)S(1)}, bf16[2,768,128]{2,1,0:T(8,128)(2,1)S(1)}, u32[]{:S(2)}, u32[]{:S(2)}) collective-permute-start(bf16[2,768,128]{2,1,0:T(8,128)(2,1)S(1)} %collective-permute-done.2.refs_2_), channel_id=1, source_target_pairs={{0,2},{1,7},{2,4},{3,1},{4,6},{5,3},{6,0},{7,5},{8,10},{9,15},{10,... | collective-permute-start | bytes 1179656 | tf_op jit(solution)/shard_map/ppermute | solution.py:24
  86.5 0.0 collective-permute-done.8.refs_2_
  86.5 3.2 %collective-permute-start.9 = (bf16[2,768,128]{2,1,0:T(8,128)(2,1)S(1)}, bf16[2,768,128]{2,1,0:T(8,128)(2,1)S(1)}, u32[]{:S(2)}, u32[]{:S(2)}) collective-permute-start(bf16[2,768,128]{2,1,0:T(8,128)(2,1)S(1)} %collective-permute-done.8.refs_2_), channel_id=1, source_target_pairs={{0,2},{1,7},{2,4},{3,1},{4,6},{5,3},{6,0},{7,5},{8,10},{9,15},{10,... | collective-permute-start | bytes 1179656 | tf_op jit(solution)/shard_map/ppermute | solution.py:24
  89.7 0.0 collective-permute-done.12.refs_1_
  89.7 2.5 %collective-permute-start.13 = (bf16[2,256,768]{2,1,0:T(8,128)(2,1)S(1)}, bf16[2,256,768]{2,1,0:T(8,128)(2,1)}, u32[]{:S(2)}, u32[]{:S(2)}) collective-permute-start(bf16[2,256,768]{2,1,0:T(8,128)(2,1)S(1)} %collective-permute-done.12.refs_1_), channel_id=1, source_target_pairs={{0,128},{1,385},{128,256},{129,1},{256,384},{257,129},{384,0},{385... | collective-permute-start | bytes 2359304 | tf_op jit(solution)/shard_map/ppermute | solution.py:24
  92.2 0.7 collective-permute-done.3.refs_3_
  92.9 0.1 shard_map.75.refs_0_
  93.0 5.8 %collective-permute-start.4 = (bf16[8,768,128]{2,1,0:T(8,128)(2,1)S(1)}, bf16[8,768,128]{2,1,0:T(8,128)(2,1)}, u32[]{:S(2)}, u32[]{:S(2)}) collective-permute-start(bf16[8,768,128]{2,1,0:T(8,128)(2,1)S(1)} %shard_map.75.refs_0_), channel_id=1, source_target_pairs={{0,1},{1,0},{2,3},{3,2},{4,5},{5,4},{6,7},{7,6},{8,9},{9,8},{10,11... | collective-permute-start | bytes 4718600 | tf_op jit(solution)/shard_map/ppermute | solution.py:28
  98.8 0.0 collective-permute-done.9.refs_3_
  98.9 0.1 shard_map.77.refs_2_
  99.0 0.0 copy-done.2
  99.0 0.0 copy-done.6
  99.0 4.1 %collective-permute-start.10 = (bf16[8,768,128]{2,1,0:T(8,128)(2,1)S(1)}, bf16[8,768,128]{2,1,0:T(8,128)(2,1)}, u32[]{:S(2)}, u32[]{:S(2)}) collective-permute-start(bf16[8,768,128]{2,1,0:T(8,128)(2,1)S(1)} %shard_map.77.refs_2_), channel_id=1, source_target_pairs={{0,1},{1,0},{2,3},{3,2},{4,5},{5,4},{6,7},{7,6},{8,9},{9,8},{10,11... | collective-permute-start | bytes 4718600 | tf_op jit(solution)/shard_map/ppermute | solution.py:28
  103.1 0.0 collective-permute-done.17.refs_6_
  103.1 3.4 %collective-permute-start.18 = (bf16[2,256,768]{2,1,0:T(8,128)(2,1)S(1)}, bf16[2,256,768]{2,1,0:T(8,128)(2,1)}, u32[]{:S(2)}, u32[]{:S(2)}) collective-permute-start(bf16[2,256,768]{2,1,0:T(8,128)(2,1)S(1)} %collective-permute-done.17.refs_6_), channel_id=1, source_target_pairs={{0,128},{1,385},{128,256},{129,1},{256,384},{257,129},{384,0},{385... | collective-permute-start | bytes 2359304 | tf_op jit(solution)/shard_map/ppermute | solution.py:24
  106.5 0.0 copy-start.8
  106.5 0.9 copy-done.8
  107.4 0.0 collective-permute-done.13.refs_2_
  107.4 3.2 %collective-permute-start.14 = (bf16[2,256,768]{2,1,0:T(8,128)(2,1)}, bf16[2,256,768]{2,1,0:T(8,128)(2,1)}, u32[]{:S(2)}, u32[]{:S(2)}) collective-permute-start(bf16[2,256,768]{2,1,0:T(8,128)(2,1)} %collective-permute-done.13.refs_2_), channel_id=1, source_target_pairs={{0,128},{1,385},{128,256},{129,1},{256,384},{257,129},{384,0},{385... | collective-permute-start | bytes 2359304 | tf_op jit(solution)/shard_map/ppermute | solution.py:24
  110.5 5.7 %collective-permute-done.18.refs_7_ = bf16[2,256,768]{2,1,0:T(8,128)(2,1)} collective-permute-done((bf16[2,256,768]{2,1,0:T(8,128)(2,1)S(1)}, bf16[2,256,768]{2,1,0:T(8,128)(2,1)}, u32[]{:S(2)}, u32[]{:S(2)}) %collective-permute-start.18) | collective-permute-done | bytes 786464 | tf_op jit(solution)/shard_map/ppermute | solution.py:24
  116.2 4.3 %collective-permute-start.19 = (bf16[2,256,768]{2,1,0:T(8,128)(2,1)}, bf16[2,256,768]{2,1,0:T(8,128)(2,1)}, u32[]{:S(2)}, u32[]{:S(2)}) collective-permute-start(bf16[2,256,768]{2,1,0:T(8,128)(2,1)} %collective-permute-done.18.refs_7_), channel_id=1, source_target_pairs={{0,128},{1,385},{128,256},{129,1},{256,384},{257,129},{384,0},{385... | collective-permute-start | bytes 2359304 | tf_op jit(solution)/shard_map/ppermute | solution.py:24
  120.5 0.1 stack.23.at_ref
  120.6 4.0 %collective-permute-done.14.refs_3_ = bf16[2,256,768]{2,1,0:T(8,128)(2,1)} collective-permute-done((bf16[2,256,768]{2,1,0:T(8,128)(2,1)}, bf16[2,256,768]{2,1,0:T(8,128)(2,1)}, u32[]{:S(2)}, u32[]{:S(2)}) %collective-permute-start.14) | collective-permute-done | bytes 786464 | tf_op jit(solution)/shard_map/ppermute | solution.py:24
  124.6 1.1 copy-done.1
  125.8 1.1 copy-done.7
  126.9 1.7 shard_map.79.refs_4_
  128.6 0.0 collective-permute-done.4.refs_1_
  128.6 0.0 collective-permute-done.10.refs_3_
  128.6 4.4 %collective-permute-done.19.refs_8_ = bf16[2,256,768]{2,1,0:T(8,128)(2,1)} collective-permute-done((bf16[2,256,768]{2,1,0:T(8,128)(2,1)}, bf16[2,256,768]{2,1,0:T(8,128)(2,1)}, u32[]{:S(2)}, u32[]{:S(2)}) %collective-permute-start.19) | collective-permute-done | bytes 786464 | tf_op jit(solution)/shard_map/ppermute | solution.py:24
  133.1 8.5 %shard_map.81 = (f32[768,768]{1,0:T(8,128)S(1)}, f32[6,128]{1,0:T(8,128)S(1)}) custom-call(s32[5]{0:T(128)S(1)} %stack.23.at_ref, s32[6,6]{1,0:T(8,128)S(1)} %copy-done.12, bf16[8,768,128]{2,1,0:T(8,128)(2,1)S(1)} %shard_map.75.refs_0_, bf16[8,768,128]{2,1,0:T(8,128)(2,1)} %collective-permute-done.4.refs_1_, bf16[8,768,128]{2,1,0:T(8,128)(2,1)S(1)} %shard_map.77.refs_2_, ...), custom_call_target="tpu_custom_call" | custom-call | tf_op jit(solution)/shard_map/pallas_call | solution.py:155
  141.6 0.0 copy-start.4
  141.6 1.4 copy-done.4
  143.0 4.2 %psum.7 = f32[768]{0:T(1024)S(1)} all-reduce(f32[768]{0:T(1024)S(1)} %bitcast.18), channel_id=1, replica_groups=mesh['x'=4,'zl'=4,'zh'=4,'y'=4,'core'=2] {'core'}, use_global_device_ids=true, to_apply=%region_0.0 | all-reduce | flops 768 | bytes 6144 | tf_op jit(solution)/shard_map/psum | solution.py:169
  147.2 22.5 %all_to_all.8 = f32[16,1,768]{2,1,0:T(1,128)S(1)} all-to-all(f32[16,1,768]{2,1,0:T(1,128)S(1)} %broadcast_in_dim.11), channel_id=1, replica_groups=mesh['x'=4,'zl'=4,'zh'=4,'y'=4,'core'=2] {'zh','y'}, dimensions={0} | all-to-all | bytes 98304 | tf_op jit(solution)/shard_map/all_to_all | solution.py:171
  169.7 1.7 copy-done.5
  171.4 1.5 shard_map.82
  (17 shorter events, 0.1 us)
Async XLA Ops:
  2.1 66.8 %copy-start.10 = (bf16[256,768]{1,0:T(8,128)(2,1)S(1)}, bf16[256,768]{1,0:T(8,128)(2,1)}, u32[]{:S(2)}) copy-start(bf16[256,768]{1,0:T(8,128)(2,1)} %get-tuple-element.10) | copy-start | bytes 1179652
  2.1 30.1 %collective-permute-start.11 = (bf16[1,256,768]{2,1,0:T(8,128)(2,1)}, bf16[1,256,768]{2,1,0:T(8,128)(2,1)S(1)}, u32[]{:S(2)}, u32[]{:S(2)}) collective-permute-start(bf16[1,256,768]{2,1,0:T(8,128)(2,1)} %bitcast.13), channel_id=1, source_target_pairs={{0,32},{1,97},{32,64},{33,1},{64,96},{65,33},{96,0},{97,65},{2,34}... | collective-permute-start | bytes 1179656 | tf_op jit(solution)/shard_map/ppermute | solution.py:24
  9.3 15.2 %collective-permute-start = (bf16[1,768,128]{2,1,0:T(8,128)(2,1)}, bf16[1,768,128]{2,1,0:T(8,128)(2,1)S(1)}, u32[]{:S(2)}, u32[]{:S(2)}) collective-permute-start(bf16[1,768,128]{2,1,0:T(8,128)(2,1)} %bitcast.16), channel_id=1, source_target_pairs={{0,8},{1,25},{8,16},{9,1},{16,24},{17,9},{24,0},{25,17},{2,10},{3,... | collective-permute-start | bytes 589832 | tf_op jit(solution)/shard_map/ppermute | solution.py:24
  24.5 14.9 %collective-permute-start.5 = (bf16[1,768,128]{2,1,0:T(8,128)(2,1)S(1)}, bf16[1,768,128]{2,1,0:T(8,128)(2,1)S(1)}, u32[]{:S(2)}, u32[]{:S(2)}) collective-permute-start(bf16[1,768,128]{2,1,0:T(8,128)(2,1)S(1)} %collective-permute-done.refs_1_), channel_id=1, source_target_pairs={{0,8},{1,25},{8,16},{9,1},{16,24},{17,9},{24,0},{25,17},{2,10},{3,... | collective-permute-start | bytes 589832 | tf_op jit(solution)/shard_map/ppermute | solution.py:24
  32.2 26.8 %collective-permute-start.15 = (bf16[1,256,768]{2,1,0:T(8,128)(2,1)S(1)}, bf16[1,256,768]{2,1,0:T(8,128)(2,1)S(1)}, u32[]{:S(2)}, u32[]{:S(2)}) collective-permute-start(bf16[1,256,768]{2,1,0:T(8,128)(2,1)S(1)} %collective-permute-done.11.refs_1_), channel_id=1, source_target_pairs={{0,32},{1,97},{32,64},{33,1},{64,96},{65,33},{96,0},{97,65},{2,34}... | collective-permute-start | bytes 1179656 | tf_op jit(solution)/shard_map/ppermute | solution.py:24
  39.4 17.2 %collective-permute-start.6 = (bf16[1,768,128]{2,1,0:T(8,128)(2,1)S(1)}, bf16[1,768,128]{2,1,0:T(8,128)(2,1)S(1)}, u32[]{:S(2)}, u32[]{:S(2)}) collective-permute-start(bf16[1,768,128]{2,1,0:T(8,128)(2,1)S(1)} %collective-permute-done.5.refs_0_), channel_id=1, source_target_pairs={{0,8},{1,25},{8,16},{9,1},{16,24},{17,9},{24,0},{25,17},{2,10},{3,... | collective-permute-start | bytes 589832 | tf_op jit(solution)/shard_map/ppermute | solution.py:24
  47.0 0.9 copy-start.11
  48.0 25.4 %collective-permute-start.1 = (bf16[2,768,128]{2,1,0:T(8,128)(2,1)S(1)}, bf16[2,768,128]{2,1,0:T(8,128)(2,1)S(1)}, u32[]{:S(2)}, u32[]{:S(2)}) collective-permute-start(bf16[2,768,128]{2,1,0:T(8,128)(2,1)S(1)} %shard_map.74.refs_0_), channel_id=1, source_target_pairs={{0,2},{1,7},{2,4},{3,1},{4,6},{5,3},{6,0},{7,5},{8,10},{9,15},{10,... | collective-permute-start | bytes 1179656 | tf_op jit(solution)/shard_map/ppermute | solution.py:24
  56.7 19.1 %collective-permute-start.7 = (bf16[2,768,128]{2,1,0:T(8,128)(2,1)S(1)}, bf16[2,768,128]{2,1,0:T(8,128)(2,1)S(1)}, u32[]{:S(2)}, u32[]{:S(2)}) collective-permute-start(bf16[2,768,128]{2,1,0:T(8,128)(2,1)S(1)} %shard_map.76.refs_0_), channel_id=1, source_target_pairs={{0,2},{1,7},{2,4},{3,1},{4,6},{5,3},{6,0},{7,5},{8,10},{9,15},{10,... | collective-permute-start | bytes 1179656 | tf_op jit(solution)/shard_map/ppermute | solution.py:24
  59.1 20.6 %collective-permute-start.16 = (bf16[1,256,768]{2,1,0:T(8,128)(2,1)S(1)}, bf16[1,256,768]{2,1,0:T(8,128)(2,1)S(1)}, u32[]{:S(2)}, u32[]{:S(2)}) collective-permute-start(bf16[1,256,768]{2,1,0:T(8,128)(2,1)S(1)} %collective-permute-done.15.refs_0_), channel_id=1, source_target_pairs={{0,32},{1,97},{32,64},{33,1},{64,96},{65,33},{96,0},{97,65},{2,34}... | collective-permute-start | bytes 1179656 | tf_op jit(solution)/shard_map/ppermute | solution.py:24
  69.0 24.0 %copy-start = (bf16[2,256,768]{2,1,0:T(8,128)(2,1)}, bf16[2,256,768]{2,1,0:T(8,128)(2,1)S(1)}, u32[]{:S(2)}) copy-start(bf16[2,256,768]{2,1,0:T(8,128)(2,1)S(1)} %shard_map.78.refs_0_) | copy-start | bytes 2359300
  69.0 20.7 %collective-permute-start.12 = (bf16[2,256,768]{2,1,0:T(8,128)(2,1)S(1)}, bf16[2,256,768]{2,1,0:T(8,128)(2,1)S(1)}, u32[]{:S(2)}, u32[]{:S(2)}) collective-permute-start(bf16[2,256,768]{2,1,0:T(8,128)(2,1)S(1)} %shard_map.78.refs_0_), channel_id=1, source_target_pairs={{0,128},{1,385},{128,256},{129,1},{256,384},{257,129},{384,0},{385... | collective-permute-start | bytes 2359304 | tf_op jit(solution)/shard_map/ppermute | solution.py:24
  73.4 10.7 %collective-permute-start.2 = (bf16[2,768,128]{2,1,0:T(8,128)(2,1)S(1)}, bf16[2,768,128]{2,1,0:T(8,128)(2,1)S(1)}, u32[]{:S(2)}, u32[]{:S(2)}) collective-permute-start(bf16[2,768,128]{2,1,0:T(8,128)(2,1)S(1)} %collective-permute-done.1.refs_1_), channel_id=1, source_target_pairs={{0,2},{1,7},{2,4},{3,1},{4,6},{5,3},{6,0},{7,5},{8,10},{9,15},{10,... | collective-permute-start | bytes 1179656 | tf_op jit(solution)/shard_map/ppermute | solution.py:24
  75.8 10.7 %collective-permute-start.8 = (bf16[2,768,128]{2,1,0:T(8,128)(2,1)S(1)}, bf16[2,768,128]{2,1,0:T(8,128)(2,1)S(1)}, u32[]{:S(2)}, u32[]{:S(2)}) collective-permute-start(bf16[2,768,128]{2,1,0:T(8,128)(2,1)S(1)} %collective-permute-done.7.refs_1_), channel_id=1, source_target_pairs={{0,2},{1,7},{2,4},{3,1},{4,6},{5,3},{6,0},{7,5},{8,10},{9,15},{10,... | collective-permute-start | bytes 1179656 | tf_op jit(solution)/shard_map/ppermute | solution.py:24
  79.7 19.3 %copy-start.2 = (bf16[2,256,768]{2,1,0:T(8,128)(2,1)}, bf16[2,256,768]{2,1,0:T(8,128)(2,1)S(1)}, u32[]{:S(2)}) copy-start(bf16[2,256,768]{2,1,0:T(8,128)(2,1)S(1)} %shard_map.80.refs_5_) | copy-start | bytes 2359300
  79.7 23.4 %collective-permute-start.17 = (bf16[2,256,768]{2,1,0:T(8,128)(2,1)S(1)}, bf16[2,256,768]{2,1,0:T(8,128)(2,1)S(1)}, u32[]{:S(2)}, u32[]{:S(2)}) collective-permute-start(bf16[2,256,768]{2,1,0:T(8,128)(2,1)S(1)} %shard_map.80.refs_5_), channel_id=1, source_target_pairs={{0,128},{1,385},{128,256},{129,1},{256,384},{257,129},{384,0},{385... | collective-permute-start | bytes 2359304 | tf_op jit(solution)/shard_map/ppermute | solution.py:24
  84.1 8.8 %collective-permute-start.3 = (bf16[2,768,128]{2,1,0:T(8,128)(2,1)S(1)}, bf16[2,768,128]{2,1,0:T(8,128)(2,1)S(1)}, u32[]{:S(2)}, u32[]{:S(2)}) collective-permute-start(bf16[2,768,128]{2,1,0:T(8,128)(2,1)S(1)} %collective-permute-done.2.refs_2_), channel_id=1, source_target_pairs={{0,2},{1,7},{2,4},{3,1},{4,6},{5,3},{6,0},{7,5},{8,10},{9,15},{10,... | collective-permute-start | bytes 1179656 | tf_op jit(solution)/shard_map/ppermute | solution.py:24
  86.5 12.4 %collective-permute-start.9 = (bf16[2,768,128]{2,1,0:T(8,128)(2,1)S(1)}, bf16[2,768,128]{2,1,0:T(8,128)(2,1)S(1)}, u32[]{:S(2)}, u32[]{:S(2)}) collective-permute-start(bf16[2,768,128]{2,1,0:T(8,128)(2,1)S(1)} %collective-permute-done.8.refs_2_), channel_id=1, source_target_pairs={{0,2},{1,7},{2,4},{3,1},{4,6},{5,3},{6,0},{7,5},{8,10},{9,15},{10,... | collective-permute-start | bytes 1179656 | tf_op jit(solution)/shard_map/ppermute | solution.py:24
  89.7 9.3 %copy-start.6 = (bf16[2,256,768]{2,1,0:T(8,128)(2,1)}, bf16[2,256,768]{2,1,0:T(8,128)(2,1)S(1)}, u32[]{:S(2)}) copy-start(bf16[2,256,768]{2,1,0:T(8,128)(2,1)S(1)} %collective-permute-done.12.refs_1_) | copy-start | bytes 2359300
  89.7 17.6 %collective-permute-start.13 = (bf16[2,256,768]{2,1,0:T(8,128)(2,1)S(1)}, bf16[2,256,768]{2,1,0:T(8,128)(2,1)}, u32[]{:S(2)}, u32[]{:S(2)}) collective-permute-start(bf16[2,256,768]{2,1,0:T(8,128)(2,1)S(1)} %collective-permute-done.12.refs_1_), channel_id=1, source_target_pairs={{0,128},{1,385},{128,256},{129,1},{256,384},{257,129},{384,0},{385... | collective-permute-start | bytes 2359304 | tf_op jit(solution)/shard_map/ppermute | solution.py:24
  93.0 35.6 %collective-permute-start.4 = (bf16[8,768,128]{2,1,0:T(8,128)(2,1)S(1)}, bf16[8,768,128]{2,1,0:T(8,128)(2,1)}, u32[]{:S(2)}, u32[]{:S(2)}) collective-permute-start(bf16[8,768,128]{2,1,0:T(8,128)(2,1)S(1)} %shard_map.75.refs_0_), channel_id=1, source_target_pairs={{0,1},{1,0},{2,3},{3,2},{4,5},{5,4},{6,7},{7,6},{8,9},{9,8},{10,11... | collective-permute-start | bytes 4718600 | tf_op jit(solution)/shard_map/ppermute | solution.py:28
  99.0 29.6 %collective-permute-start.10 = (bf16[8,768,128]{2,1,0:T(8,128)(2,1)S(1)}, bf16[8,768,128]{2,1,0:T(8,128)(2,1)}, u32[]{:S(2)}, u32[]{:S(2)}) collective-permute-start(bf16[8,768,128]{2,1,0:T(8,128)(2,1)S(1)} %shard_map.77.refs_2_), channel_id=1, source_target_pairs={{0,1},{1,0},{2,3},{3,2},{4,5},{5,4},{6,7},{7,6},{8,9},{9,8},{10,11... | collective-permute-start | bytes 4718600 | tf_op jit(solution)/shard_map/ppermute | solution.py:28
  103.1 13.1 %collective-permute-start.18 = (bf16[2,256,768]{2,1,0:T(8,128)(2,1)S(1)}, bf16[2,256,768]{2,1,0:T(8,128)(2,1)}, u32[]{:S(2)}, u32[]{:S(2)}) collective-permute-start(bf16[2,256,768]{2,1,0:T(8,128)(2,1)S(1)} %collective-permute-done.17.refs_6_), channel_id=1, source_target_pairs={{0,128},{1,385},{128,256},{129,1},{256,384},{257,129},{384,0},{385... | collective-permute-start | bytes 2359304 | tf_op jit(solution)/shard_map/ppermute | solution.py:24
  106.5 0.9 copy-start.8
  107.4 17.3 %collective-permute-start.14 = (bf16[2,256,768]{2,1,0:T(8,128)(2,1)}, bf16[2,256,768]{2,1,0:T(8,128)(2,1)}, u32[]{:S(2)}, u32[]{:S(2)}) collective-permute-start(bf16[2,256,768]{2,1,0:T(8,128)(2,1)} %collective-permute-done.13.refs_2_), channel_id=1, source_target_pairs={{0,128},{1,385},{128,256},{129,1},{256,384},{257,129},{384,0},{385... | collective-permute-start | bytes 2359304 | tf_op jit(solution)/shard_map/ppermute | solution.py:24
  116.2 16.9 %collective-permute-start.19 = (bf16[2,256,768]{2,1,0:T(8,128)(2,1)}, bf16[2,256,768]{2,1,0:T(8,128)(2,1)}, u32[]{:S(2)}, u32[]{:S(2)}) collective-permute-start(bf16[2,256,768]{2,1,0:T(8,128)(2,1)} %collective-permute-done.18.refs_7_), channel_id=1, source_target_pairs={{0,128},{1,385},{128,256},{129,1},{256,384},{257,129},{384,0},{385... | collective-permute-start | bytes 2359304 | tf_op jit(solution)/shard_map/ppermute | solution.py:24
  124.6 1.1 copy-start.1
  125.8 1.1 copy-start.7
  126.9 6.2 %copy-start.3 = (bf16[2,256,768]{2,1,0:T(8,128)(2,1)S(1)}, bf16[2,256,768]{2,1,0:T(8,128)(2,1)}, u32[]{:S(2)}) copy-start(bf16[2,256,768]{2,1,0:T(8,128)(2,1)} %copy-done.2) | copy-start | bytes 2359300
  126.9 6.2 %copy-start.9 = (bf16[2,256,768]{2,1,0:T(8,128)(2,1)S(1)}, bf16[2,256,768]{2,1,0:T(8,128)(2,1)}, u32[]{:S(2)}) copy-start(bf16[2,256,768]{2,1,0:T(8,128)(2,1)} %copy-done.8) | copy-start | bytes 2359300
  126.9 6.2 %copy-start.12 = (s32[6,6]{1,0:T(8,128)S(1)}, s32[6,6]{1,0:T(8,128)}, u32[]{:S(2)}) copy-start(s32[6,6]{1,0:T(8,128)} %keep_ref.1) | copy-start | bytes 436
  141.6 1.4 copy-start.4
  169.7 1.7 copy-start.5

commit v4 on v3

--- a/solution.py
+++ b/solution.py
@@ -35,15 +35,15 @@
         at += ref.shape[0]
 
 
-def join(parts, after=()):
+def join(parts):
     shape = (sum(p.shape[0] for p in parts),) + parts[0].shape[1:]
     return pl.pallas_call(
         functools.partial(copy_parts, len(parts)),
         out_shape=jax.ShapeDtypeStruct(shape, jnp.bfloat16),
-        in_specs=[VMEM] * (len(parts) + len(after)),
+        in_specs=[VMEM] * len(parts),
         out_specs=VMEM,
         compiler_params=pltpu.CompilerParams(vmem_limit_bytes=10 * MIB),
-    )(*parts, *after)
+    )(*parts)
 
 
 def scale_tiles(*refs):
@@ -150,7 +150,7 @@
         blocks = [join(lane[first:first + 2])]
         for _ in range(SIDE - 1):
             blocks.append(step(blocks[-1], "x"))
-        rights += blocks if first else [join(blocks)]
+        rights.append(join(blocks))
     operands = [v for v, _ in lefts] + rights
     pruned, totals = pl.pallas_call(
         functools.partial(multiply, [p for _, p in lefts]),

time: 174 us -> 177 us (1.017)
  starting transfers between devices: 102 us -> 94.1 us
  blocking collectives: 26.7 us -> 32.1 us
  waiting for transfers between devices: 22 us -> 26.7 us
    ppermute x18, starting transfers between devices: 92.4 us -> 86.9 us  [step(): return lax.ppermute(value, (axis, 'core'), pairs)]
    ppermute x18, waiting for transfers between devices: 22 us -> 26.7 us  [step(): return lax.ppermute(value, (axis, 'core'), pairs)]
    all_to_all x1, blocking collectives: 22.5 us -> 26.9 us  [per_device(): shares = lax.all_to_all(spread, ('zh', 'y'), 0, 0)]
    ppermute x2, starting transfers between devices: 9.89 us -> 7.23 us  [swap(): return lax.ppermute(value, 'core', [(0, 1), (1, 0)])]
    pallas_call x7 -> x8, Pallas kernels: 2.06 us -> 3.63 us  [join(): pl.pallas_call(functools.partial(copy_parts, len(parts)), out_shape=jax.S...]
  transfers between devices with their start and end apart: 20 -> 20, of which waited for: 6 -> 8; matrix products, arithmetic and copies ran while one was open for 0% -> 0% of each run, Pallas kernels for 1% -> 2%
where the time goes in v4:
time: 177 us; the launch traced here: 176 us
  starting transfers between devices  94.1 us (53%)
  blocking collectives  32.1 us (18%)
  waiting for transfers between devices  26.7 us (15%)
  Pallas kernels  15.2 us (9%)
  local copies, waits for them, and re-layouts  7.4 us (4%)
    ppermute x18, starting transfers between devices, step(): return lax.ppermute(value, (axis, 'core'), pairs)  86.9 us
    all_to_all x1, blocking collectives, per_device(): shares = lax.all_to_all(spread, ('zh', 'y'), 0, 0)  26.9 us
    ppermute x18, waiting for transfers between devices, step(): return lax.ppermute(value, (axis, 'core'), pairs)  26.7 us
    pallas_call x1, Pallas kernels, per_device(): pl.pallas_call(functools.partial(multiply, [p for _, p in lefts]), out_sh...  7.99 us
    unnamed x27, local copies, waits for them, and re-layouts  7.28 us
    ppermute x2, starting transfers between devices, swap(): return lax.ppermute(value, 'core', [(0, 1), (1, 0)])  7.23 us
    psum x1, blocking collectives, per_device(): totals = lax.psum(totals, 'core')  5.12 us
    pallas_call x8, Pallas kernels, join(): pl.pallas_call(functools.partial(copy_parts, len(parts)), out_shape=jax.S...  3.63 us
  transfers between devices with their start and end apart: 20, of which 8 were waited for; matrix products, arithmetic and copies ran while one was open for 0% of the time, Pallas kernels for 2%

profile of v4, /device:TPU:1, one launch (start us, length us, event | category | flops | bytes accessed | tf_op | source)
XLA Modules:
  0.0 175.9 jit_solution(3712828921408901674)
XLA Ops:
  0.0 2.1 %shard_map.73 = (bf16[256,768]{1,0:T(8,128)(2,1)}, bf16[768,128]{1,0:T(8,128)(2,1)}) custom-call(f32[2,6]{1,0:T(2,128)} %refs_0_.1, s32[2,6]{1,0:T(2,128)} %refs_1_.1, bf16[256,768]{1,0:T(8,128)(2,1)} %refs_2_.1, f32[1,6]{1,0:T(1,128)} %bitcast.19, s32[1,6]{1,0:T(1,128)} %bitcast.20, bf16[768,128]{1,0:T(8,128)(2,1)} %refs_5_.1), custom_call_target="tpu_custom_call" | custom-call | tf_op jit(solution)/shard_map/pallas_call | solution.py:68
  2.1 7.1 %collective-permute-start.11 = (bf16[1,256,768]{2,1,0:T(8,128)(2,1)}, bf16[1,256,768]{2,1,0:T(8,128)(2,1)S(1)}, u32[]{:S(2)}, u32[]{:S(2)}) collective-permute-start(bf16[1,256,768]{2,1,0:T(8,128)(2,1)} %bitcast.13), channel_id=1, source_target_pairs={{0,32},{1,97},{32,64},{33,1},{64,96},{65,33},{96,0},{97,65},{2,34}... | collective-permute-start | bytes 1179656 | tf_op jit(solution)/shard_map/ppermute | solution.py:24
  9.2 9.8 %collective-permute-start = (bf16[1,768,128]{2,1,0:T(8,128)(2,1)}, bf16[1,768,128]{2,1,0:T(8,128)(2,1)S(1)}, u32[]{:S(2)}, u32[]{:S(2)}) collective-permute-start(bf16[1,768,128]{2,1,0:T(8,128)(2,1)} %bitcast.16), channel_id=1, source_target_pairs={{0,8},{1,25},{8,16},{9,1},{16,24},{17,9},{24,0},{25,17},{2,10},{3,... | collective-permute-start | bytes 589832 | tf_op jit(solution)/shard_map/ppermute | solution.py:24
  18.9 0.0 collective-permute-done.11.refs_1_
  18.9 3.1 %collective-permute-start.15 = (bf16[1,256,768]{2,1,0:T(8,128)(2,1)S(1)}, bf16[1,256,768]{2,1,0:T(8,128)(2,1)S(1)}, u32[]{:S(2)}, u32[]{:S(2)}) collective-permute-start(bf16[1,256,768]{2,1,0:T(8,128)(2,1)S(1)} %collective-permute-done.11.refs_1_), channel_id=1, source_target_pairs={{0,32},{1,97},{32,64},{33,1},{64,96},{65,33},{96,0},{97,65},{2,34}... | collective-permute-start | bytes 1179656 | tf_op jit(solution)/shard_map/ppermute | solution.py:24
  22.0 2.3 %collective-permute-done.refs_1_ = bf16[1,768,128]{2,1,0:T(8,128)(2,1)S(1)} collective-permute-done((bf16[1,768,128]{2,1,0:T(8,128)(2,1)}, bf16[1,768,128]{2,1,0:T(8,128)(2,1)S(1)}, u32[]{:S(2)}, u32[]{:S(2)}) %collective-permute-start) | collective-permute-done | bytes 196640 | tf_op jit(solution)/shard_map/ppermute | solution.py:24
  24.3 11.2 %collective-permute-start.5 = (bf16[1,768,128]{2,1,0:T(8,128)(2,1)S(1)}, bf16[1,768,128]{2,1,0:T(8,128)(2,1)S(1)}, u32[]{:S(2)}, u32[]{:S(2)}) collective-permute-start(bf16[1,768,128]{2,1,0:T(8,128)(2,1)S(1)} %collective-permute-done.refs_1_), channel_id=1, source_target_pairs={{0,8},{1,25},{8,16},{9,1},{16,24},{17,9},{24,0},{25,17},{2,10},{3,... | collective-permute-start | bytes 589832 | tf_op jit(solution)/shard_map/ppermute | solution.py:24
  35.5 4.2 %collective-permute-done.5.refs_0_ = bf16[1,768,128]{2,1,0:T(8,128)(2,1)S(1)} collective-permute-done((bf16[1,768,128]{2,1,0:T(8,128)(2,1)S(1)}, bf16[1,768,128]{2,1,0:T(8,128)(2,1)S(1)}, u32[]{:S(2)}, u32[]{:S(2)}) %collective-permute-start.5) | collective-permute-done | bytes 196640 | tf_op jit(solution)/shard_map/ppermute | solution.py:24
  39.8 6.9 %collective-permute-start.6 = (bf16[1,768,128]{2,1,0:T(8,128)(2,1)S(1)}, bf16[1,768,128]{2,1,0:T(8,128)(2,1)S(1)}, u32[]{:S(2)}, u32[]{:S(2)}) collective-permute-start(bf16[1,768,128]{2,1,0:T(8,128)(2,1)S(1)} %collective-permute-done.5.refs_0_), channel_id=1, source_target_pairs={{0,8},{1,25},{8,16},{9,1},{16,24},{17,9},{24,0},{25,17},{2,10},{3,... | collective-permute-start | bytes 589832 | tf_op jit(solution)/shard_map/ppermute | solution.py:24
  46.7 0.0 copy-start.11
  46.7 0.9 copy-done.11
  47.7 10.6 %collective-permute-start.1 = (bf16[2,768,128]{2,1,0:T(8,128)(2,1)S(1)}, bf16[2,768,128]{2,1,0:T(8,128)(2,1)S(1)}, u32[]{:S(2)}, u32[]{:S(2)}) collective-permute-start(bf16[2,768,128]{2,1,0:T(8,128)(2,1)S(1)} %shard_map.74.refs_0_), channel_id=1, source_target_pairs={{0,2},{1,7},{2,4},{3,1},{4,6},{5,3},{6,0},{7,5},{8,10},{9,15},{10,... | collective-permute-start | bytes 1179656 | tf_op jit(solution)/shard_map/ppermute | solution.py:24
  58.3 0.0 collective-permute-done.15.refs_0_
  58.3 3.4 %collective-permute-start.16 = (bf16[1,256,768]{2,1,0:T(8,128)(2,1)S(1)}, bf16[1,256,768]{2,1,0:T(8,128)(2,1)S(1)}, u32[]{:S(2)}, u32[]{:S(2)}) collective-permute-start(bf16[1,256,768]{2,1,0:T(8,128)(2,1)S(1)} %collective-permute-done.15.refs_0_), channel_id=1, source_target_pairs={{0,32},{1,97},{32,64},{33,1},{64,96},{65,33},{96,0},{97,65},{2,34}... | collective-permute-start | bytes 1179656 | tf_op jit(solution)/shard_map/ppermute | solution.py:24
  61.7 0.0 collective-permute-done.6.refs_1_
  61.8 2.4 %collective-permute-start.7 = (bf16[2,768,128]{2,1,0:T(8,128)(2,1)S(1)}, bf16[2,768,128]{2,1,0:T(8,128)(2,1)S(1)}, u32[]{:S(2)}, u32[]{:S(2)}) collective-permute-start(bf16[2,768,128]{2,1,0:T(8,128)(2,1)S(1)} %shard_map.76.refs_0_), channel_id=1, source_target_pairs={{0,2},{1,7},{2,4},{3,1},{4,6},{5,3},{6,0},{7,5},{8,10},{9,15},{10,... | collective-permute-start | bytes 1179656 | tf_op jit(solution)/shard_map/ppermute | solution.py:24
  64.1 0.0 copy-start.10
  64.1 1.0 copy-done.10
  65.1 0.1 shard_map.78.refs_0_
  65.2 0.0 copy-start
  65.2 4.4 %collective-permute-start.12 = (bf16[2,256,768]{2,1,0:T(8,128)(2,1)S(1)}, bf16[2,256,768]{2,1,0:T(8,128)(2,1)S(1)}, u32[]{:S(2)}, u32[]{:S(2)}) collective-permute-start(bf16[2,256,768]{2,1,0:T(8,128)(2,1)S(1)} %shard_map.78.refs_0_), channel_id=1, source_target_pairs={{0,128},{1,385},{128,256},{129,1},{256,384},{257,129},{384,0},{385... | collective-permute-start | bytes 2359304 | tf_op jit(solution)/shard_map/ppermute | solution.py:24
  69.6 0.0 collective-permute-done.1.refs_1_
  69.6 2.1 %collective-permute-start.2 = (bf16[2,768,128]{2,1,0:T(8,128)(2,1)S(1)}, bf16[2,768,128]{2,1,0:T(8,128)(2,1)S(1)}, u32[]{:S(2)}, u32[]{:S(2)}) collective-permute-start(bf16[2,768,128]{2,1,0:T(8,128)(2,1)S(1)} %collective-permute-done.1.refs_1_), channel_id=1, source_target_pairs={{0,2},{1,7},{2,4},{3,1},{4,6},{5,3},{6,0},{7,5},{8,10},{9,15},{10,... | collective-permute-start | bytes 1179656 | tf_op jit(solution)/shard_map/ppermute | solution.py:24
  71.7 1.0 collective-permute-done.16.refs_1_
  72.6 0.1 shard_map.80.refs_0_
  72.7 0.0 copy-start.2
  72.7 4.5 %collective-permute-start.17 = (bf16[2,256,768]{2,1,0:T(8,128)(2,1)S(1)}, bf16[2,256,768]{2,1,0:T(8,128)(2,1)S(1)}, u32[]{:S(2)}, u32[]{:S(2)}) collective-permute-start(bf16[2,256,768]{2,1,0:T(8,128)(2,1)S(1)} %shard_map.80.refs_0_), channel_id=1, source_target_pairs={{0,128},{1,385},{128,256},{129,1},{256,384},{257,129},{384,0},{385... | collective-permute-start | bytes 2359304 | tf_op jit(solution)/shard_map/ppermute | solution.py:24
  77.3 0.0 collective-permute-done.7.refs_1_
  77.3 3.8 %collective-permute-start.8 = (bf16[2,768,128]{2,1,0:T(8,128)(2,1)S(1)}, bf16[2,768,128]{2,1,0:T(8,128)(2,1)S(1)}, u32[]{:S(2)}, u32[]{:S(2)}) collective-permute-start(bf16[2,768,128]{2,1,0:T(8,128)(2,1)S(1)} %collective-permute-done.7.refs_1_), channel_id=1, source_target_pairs={{0,2},{1,7},{2,4},{3,1},{4,6},{5,3},{6,0},{7,5},{8,10},{9,15},{10,... | collective-permute-start | bytes 1179656 | tf_op jit(solution)/shard_map/ppermute | solution.py:24
  81.1 0.0 collective-permute-done.2.refs_2_
  81.1 2.1 %collective-permute-start.3 = (bf16[2,768,128]{2,1,0:T(8,128)(2,1)S(1)}, bf16[2,768,128]{2,1,0:T(8,128)(2,1)S(1)}, u32[]{:S(2)}, u32[]{:S(2)}) collective-permute-start(bf16[2,768,128]{2,1,0:T(8,128)(2,1)S(1)} %collective-permute-done.2.refs_2_), channel_id=1, source_target_pairs={{0,2},{1,7},{2,4},{3,1},{4,6},{5,3},{6,0},{7,5},{8,10},{9,15},{10,... | collective-permute-start | bytes 1179656 | tf_op jit(solution)/shard_map/ppermute | solution.py:24
  83.2 2.9 %collective-permute-done.8.refs_2_ = bf16[2,768,128]{2,1,0:T(8,128)(2,1)S(1)} collective-permute-done((bf16[2,768,128]{2,1,0:T(8,128)(2,1)S(1)}, bf16[2,768,128]{2,1,0:T(8,128)(2,1)S(1)}, u32[]{:S(2)}, u32[]{:S(2)}) %collective-permute-start.8) | collective-permute-done | bytes 393248 | tf_op jit(solution)/shard_map/ppermute | solution.py:24
  86.1 5.0 %collective-permute-start.9 = (bf16[2,768,128]{2,1,0:T(8,128)(2,1)S(1)}, bf16[2,768,128]{2,1,0:T(8,128)(2,1)S(1)}, u32[]{:S(2)}, u32[]{:S(2)}) collective-permute-start(bf16[2,768,128]{2,1,0:T(8,128)(2,1)S(1)} %collective-permute-done.8.refs_2_), channel_id=1, source_target_pairs={{0,2},{1,7},{2,4},{3,1},{4,6},{5,3},{6,0},{7,5},{8,10},{9,15},{10,... | collective-permute-start | bytes 1179656 | tf_op jit(solution)/shard_map/ppermute | solution.py:24
  91.1 0.0 collective-permute-done.12.refs_1_
  91.1 2.2 %collective-permute-start.13 = (bf16[2,256,768]{2,1,0:T(8,128)(2,1)S(1)}, bf16[2,256,768]{2,1,0:T(8,128)(2,1)}, u32[]{:S(2)}, u32[]{:S(2)}) collective-permute-start(bf16[2,256,768]{2,1,0:T(8,128)(2,1)S(1)} %collective-permute-done.12.refs_1_), channel_id=1, source_target_pairs={{0,128},{1,385},{128,256},{129,1},{256,384},{257,129},{384,0},{385... | collective-permute-start | bytes 2359304 | tf_op jit(solution)/shard_map/ppermute | solution.py:24
  93.3 0.0 collective-permute-done.3.refs_3_
  93.3 0.1 shard_map.75.refs_0_
  93.4 0.0 collective-permute-done.17.refs_1_
  93.5 2.2 %collective-permute-start.18 = (bf16[2,256,768]{2,1,0:T(8,128)(2,1)S(1)}, bf16[2,256,768]{2,1,0:T(8,128)(2,1)}, u32[]{:S(2)}, u32[]{:S(2)}) collective-permute-start(bf16[2,256,768]{2,1,0:T(8,128)(2,1)S(1)} %collective-permute-done.17.refs_1_), channel_id=1, source_target_pairs={{0,128},{1,385},{128,256},{129,1},{256,384},{257,129},{384,0},{385... | collective-permute-start | bytes 2359304 | tf_op jit(solution)/shard_map/ppermute | solution.py:24
  95.6 4.0 %collective-permute-start.4 = (bf16[8,768,128]{2,1,0:T(8,128)(2,1)S(1)}, bf16[8,768,128]{2,1,0:T(8,128)(2,1)}, u32[]{:S(2)}, u32[]{:S(2)}) collective-permute-start(bf16[8,768,128]{2,1,0:T(8,128)(2,1)S(1)} %shard_map.75.refs_0_), channel_id=1, source_target_pairs={{0,1},{1,0},{2,3},{3,2},{4,5},{5,4},{6,7},{7,6},{8,9},{9,8},{10,11... | collective-permute-start | bytes 4718600 | tf_op jit(solution)/shard_map/ppermute | solution.py:28
  99.7 0.0 collective-permute-done.9.refs_3_
  99.7 0.1 shard_map.77.refs_2_
  99.8 3.2 %collective-permute-start.10 = (bf16[8,768,128]{2,1,0:T(8,128)(2,1)S(1)}, bf16[8,768,128]{2,1,0:T(8,128)(2,1)}, u32[]{:S(2)}, u32[]{:S(2)}) collective-permute-start(bf16[8,768,128]{2,1,0:T(8,128)(2,1)S(1)} %shard_map.77.refs_2_), channel_id=1, source_target_pairs={{0,1},{1,0},{2,3},{3,2},{4,5},{5,4},{6,7},{7,6},{8,9},{9,8},{10,11... | collective-permute-start | bytes 4718600 | tf_op jit(solution)/shard_map/ppermute | solution.py:28
  103.0 1.3 collective-permute-done.13.refs_2_
  104.3 3.1 %collective-permute-start.14 = (bf16[2,256,768]{2,1,0:T(8,128)(2,1)}, bf16[2,256,768]{2,1,0:T(8,128)(2,1)}, u32[]{:S(2)}, u32[]{:S(2)}) collective-permute-start(bf16[2,256,768]{2,1,0:T(8,128)(2,1)} %collective-permute-done.13.refs_2_), channel_id=1, source_target_pairs={{0,128},{1,385},{128,256},{129,1},{256,384},{257,129},{384,0},{385... | collective-permute-start | bytes 2359304 | tf_op jit(solution)/shard_map/ppermute | solution.py:24
  107.4 5.3 %collective-permute-done.18.refs_2_ = bf16[2,256,768]{2,1,0:T(8,128)(2,1)} collective-permute-done((bf16[2,256,768]{2,1,0:T(8,128)(2,1)S(1)}, bf16[2,256,768]{2,1,0:T(8,128)(2,1)}, u32[]{:S(2)}, u32[]{:S(2)}) %collective-permute-start.18) | collective-permute-done | bytes 786464 | tf_op jit(solution)/shard_map/ppermute | solution.py:24
  112.7 3.1 %collective-permute-start.19 = (bf16[2,256,768]{2,1,0:T(8,128)(2,1)}, bf16[2,256,768]{2,1,0:T(8,128)(2,1)}, u32[]{:S(2)}, u32[]{:S(2)}) collective-permute-start(bf16[2,256,768]{2,1,0:T(8,128)(2,1)} %collective-permute-done.18.refs_2_), channel_id=1, source_target_pairs={{0,128},{1,385},{128,256},{129,1},{256,384},{257,129},{384,0},{385... | collective-permute-start | bytes 2359304 | tf_op jit(solution)/shard_map/ppermute | solution.py:24
  115.8 0.1 stack.23.at_ref
  115.9 5.3 %collective-permute-done.14.refs_3_ = bf16[2,256,768]{2,1,0:T(8,128)(2,1)} collective-permute-done((bf16[2,256,768]{2,1,0:T(8,128)(2,1)}, bf16[2,256,768]{2,1,0:T(8,128)(2,1)}, u32[]{:S(2)}, u32[]{:S(2)}) %collective-permute-start.14) | collective-permute-done | bytes 786464 | tf_op jit(solution)/shard_map/ppermute | solution.py:24
  121.1 1.1 copy-done.1
  122.3 1.1 copy-done.7
  123.4 1.7 shard_map.79.refs_4_
  125.1 0.0 copy-start.12
  125.1 4.4 %collective-permute-done.19.refs_3_ = bf16[2,256,768]{2,1,0:T(8,128)(2,1)} collective-permute-done((bf16[2,256,768]{2,1,0:T(8,128)(2,1)}, bf16[2,256,768]{2,1,0:T(8,128)(2,1)}, u32[]{:S(2)}, u32[]{:S(2)}) %collective-permute-start.19) | collective-permute-done | bytes 786464 | tf_op jit(solution)/shard_map/ppermute | solution.py:24
  129.6 1.6 shard_map.81.refs_5_
  131.1 0.0 collective-permute-done.4.refs_1_
  131.2 0.0 collective-permute-done.10.refs_3_
  131.2 8.0 %shard_map.82 = (f32[768,768]{1,0:T(8,128)S(1)}, f32[6,128]{1,0:T(8,128)S(1)}) custom-call(s32[5]{0:T(128)S(1)} %stack.23.at_ref, s32[6,6]{1,0:T(8,128)S(1)} %copy-done.12, bf16[8,768,128]{2,1,0:T(8,128)(2,1)S(1)} %shard_map.75.refs_0_, bf16[8,768,128]{2,1,0:T(8,128)(2,1)} %collective-permute-done.4.refs_1_, bf16[8,768,128]{2,1,0:T(8,128)(2,1)S(1)} %shard_map.77.refs_2_, ...), custom_call_target="tpu_custom_call" | custom-call | tf_op jit(solution)/shard_map/pallas_call | solution.py:155
  139.2 0.0 copy-start.4
  139.2 1.4 copy-done.4
  140.6 5.1 %psum.7 = f32[768]{0:T(1024)S(1)} all-reduce(f32[768]{0:T(1024)S(1)} %bitcast.18), channel_id=1, replica_groups=mesh['x'=4,'zl'=4,'zh'=4,'y'=4,'core'=2] {'core'}, use_global_device_ids=true, to_apply=%region_0.0 | all-reduce | flops 768 | bytes 6144 | tf_op jit(solution)/shard_map/psum | solution.py:169
  145.7 26.9 %all_to_all.8 = f32[16,1,768]{2,1,0:T(1,128)S(1)} all-to-all(f32[16,1,768]{2,1,0:T(1,128)S(1)} %broadcast_in_dim.11), channel_id=1, replica_groups=mesh['x'=4,'zl'=4,'zh'=4,'y'=4,'core'=2] {'zh','y'}, dimensions={0} | all-to-all | bytes 98304 | tf_op jit(solution)/shard_map/all_to_all | solution.py:171
  172.7 1.7 copy-done.5
  174.3 1.5 shard_map.83
  (18 shorter events, 0.1 us)
Async XLA Ops:
  2.1 16.9 %collective-permute-start.11 = (bf16[1,256,768]{2,1,0:T(8,128)(2,1)}, bf16[1,256,768]{2,1,0:T(8,128)(2,1)S(1)}, u32[]{:S(2)}, u32[]{:S(2)}) collective-permute-start(bf16[1,256,768]{2,1,0:T(8,128)(2,1)} %bitcast.13), channel_id=1, source_target_pairs={{0,32},{1,97},{32,64},{33,1},{64,96},{65,33},{96,0},{97,65},{2,34}... | collective-permute-start | bytes 1179656 | tf_op jit(solution)/shard_map/ppermute | solution.py:24
  9.2 15.2 %collective-permute-start = (bf16[1,768,128]{2,1,0:T(8,128)(2,1)}, bf16[1,768,128]{2,1,0:T(8,128)(2,1)S(1)}, u32[]{:S(2)}, u32[]{:S(2)}) collective-permute-start(bf16[1,768,128]{2,1,0:T(8,128)(2,1)} %bitcast.16), channel_id=1, source_target_pairs={{0,8},{1,25},{8,16},{9,1},{16,24},{17,9},{24,0},{25,17},{2,10},{3,... | collective-permute-start | bytes 589832 | tf_op jit(solution)/shard_map/ppermute | solution.py:24
  18.9 39.4 %collective-permute-start.15 = (bf16[1,256,768]{2,1,0:T(8,128)(2,1)S(1)}, bf16[1,256,768]{2,1,0:T(8,128)(2,1)S(1)}, u32[]{:S(2)}, u32[]{:S(2)}) collective-permute-start(bf16[1,256,768]{2,1,0:T(8,128)(2,1)S(1)} %collective-permute-done.11.refs_1_), channel_id=1, source_target_pairs={{0,32},{1,97},{32,64},{33,1},{64,96},{65,33},{96,0},{97,65},{2,34}... | collective-permute-start | bytes 1179656 | tf_op jit(solution)/shard_map/ppermute | solution.py:24
  24.3 15.4 %collective-permute-start.5 = (bf16[1,768,128]{2,1,0:T(8,128)(2,1)S(1)}, bf16[1,768,128]{2,1,0:T(8,128)(2,1)S(1)}, u32[]{:S(2)}, u32[]{:S(2)}) collective-permute-start(bf16[1,768,128]{2,1,0:T(8,128)(2,1)S(1)} %collective-permute-done.refs_1_), channel_id=1, source_target_pairs={{0,8},{1,25},{8,16},{9,1},{16,24},{17,9},{24,0},{25,17},{2,10},{3,... | collective-permute-start | bytes 589832 | tf_op jit(solution)/shard_map/ppermute | solution.py:24
  39.8 22.0 %collective-permute-start.6 = (bf16[1,768,128]{2,1,0:T(8,128)(2,1)S(1)}, bf16[1,768,128]{2,1,0:T(8,128)(2,1)S(1)}, u32[]{:S(2)}, u32[]{:S(2)}) collective-permute-start(bf16[1,768,128]{2,1,0:T(8,128)(2,1)S(1)} %collective-permute-done.5.refs_0_), channel_id=1, source_target_pairs={{0,8},{1,25},{8,16},{9,1},{16,24},{17,9},{24,0},{25,17},{2,10},{3,... | collective-permute-start | bytes 589832 | tf_op jit(solution)/shard_map/ppermute | solution.py:24
  46.7 0.9 copy-start.11
  47.7 21.9 %collective-permute-start.1 = (bf16[2,768,128]{2,1,0:T(8,128)(2,1)S(1)}, bf16[2,768,128]{2,1,0:T(8,128)(2,1)S(1)}, u32[]{:S(2)}, u32[]{:S(2)}) collective-permute-start(bf16[2,768,128]{2,1,0:T(8,128)(2,1)S(1)} %shard_map.74.refs_0_), channel_id=1, source_target_pairs={{0,2},{1,7},{2,4},{3,1},{4,6},{5,3},{6,0},{7,5},{8,10},{9,15},{10,... | collective-permute-start | bytes 1179656 | tf_op jit(solution)/shard_map/ppermute | solution.py:24
  58.3 14.3 %collective-permute-start.16 = (bf16[1,256,768]{2,1,0:T(8,128)(2,1)S(1)}, bf16[1,256,768]{2,1,0:T(8,128)(2,1)S(1)}, u32[]{:S(2)}, u32[]{:S(2)}) collective-permute-start(bf16[1,256,768]{2,1,0:T(8,128)(2,1)S(1)} %collective-permute-done.15.refs_0_), channel_id=1, source_target_pairs={{0,32},{1,97},{32,64},{33,1},{64,96},{65,33},{96,0},{97,65},{2,34}... | collective-permute-start | bytes 1179656 | tf_op jit(solution)/shard_map/ppermute | solution.py:24
  61.8 15.5 %collective-permute-start.7 = (bf16[2,768,128]{2,1,0:T(8,128)(2,1)S(1)}, bf16[2,768,128]{2,1,0:T(8,128)(2,1)S(1)}, u32[]{:S(2)}, u32[]{:S(2)}) collective-permute-start(bf16[2,768,128]{2,1,0:T(8,128)(2,1)S(1)} %shard_map.76.refs_0_), channel_id=1, source_target_pairs={{0,2},{1,7},{2,4},{3,1},{4,6},{5,3},{6,0},{7,5},{8,10},{9,15},{10,... | collective-permute-start | bytes 1179656 | tf_op jit(solution)/shard_map/ppermute | solution.py:24
  64.1 1.0 copy-start.10
  65.2 34.6 %copy-start = (bf16[2,256,768]{2,1,0:T(8,128)(2,1)}, bf16[2,256,768]{2,1,0:T(8,128)(2,1)S(1)}, u32[]{:S(2)}) copy-start(bf16[2,256,768]{2,1,0:T(8,128)(2,1)S(1)} %shard_map.78.refs_0_) | copy-start | bytes 2359300
  65.2 25.9 %collective-permute-start.12 = (bf16[2,256,768]{2,1,0:T(8,128)(2,1)S(1)}, bf16[2,256,768]{2,1,0:T(8,128)(2,1)S(1)}, u32[]{:S(2)}, u32[]{:S(2)}) collective-permute-start(bf16[2,256,768]{2,1,0:T(8,128)(2,1)S(1)} %shard_map.78.refs_0_), channel_id=1, source_target_pairs={{0,128},{1,385},{128,256},{129,1},{256,384},{257,129},{384,0},{385... | collective-permute-start | bytes 2359304 | tf_op jit(solution)/shard_map/ppermute | solution.py:24
  69.6 11.5 %collective-permute-start.2 = (bf16[2,768,128]{2,1,0:T(8,128)(2,1)S(1)}, bf16[2,768,128]{2,1,0:T(8,128)(2,1)S(1)}, u32[]{:S(2)}, u32[]{:S(2)}) collective-permute-start(bf16[2,768,128]{2,1,0:T(8,128)(2,1)S(1)} %collective-permute-done.1.refs_1_), channel_id=1, source_target_pairs={{0,2},{1,7},{2,4},{3,1},{4,6},{5,3},{6,0},{7,5},{8,10},{9,15},{10,... | collective-permute-start | bytes 1179656 | tf_op jit(solution)/shard_map/ppermute | solution.py:24
  72.7 27.1 %copy-start.2 = (bf16[2,256,768]{2,1,0:T(8,128)(2,1)}, bf16[2,256,768]{2,1,0:T(8,128)(2,1)S(1)}, u32[]{:S(2)}) copy-start(bf16[2,256,768]{2,1,0:T(8,128)(2,1)S(1)} %shard_map.80.refs_0_) | copy-start | bytes 2359300
  72.7 20.7 %collective-permute-start.17 = (bf16[2,256,768]{2,1,0:T(8,128)(2,1)S(1)}, bf16[2,256,768]{2,1,0:T(8,128)(2,1)S(1)}, u32[]{:S(2)}, u32[]{:S(2)}) collective-permute-start(bf16[2,256,768]{2,1,0:T(8,128)(2,1)S(1)} %shard_map.80.refs_0_), channel_id=1, source_target_pairs={{0,128},{1,385},{128,256},{129,1},{256,384},{257,129},{384,0},{385... | collective-permute-start | bytes 2359304 | tf_op jit(solution)/shard_map/ppermute | solution.py:24
  77.3 8.8 %collective-permute-start.8 = (bf16[2,768,128]{2,1,0:T(8,128)(2,1)S(1)}, bf16[2,768,128]{2,1,0:T(8,128)(2,1)S(1)}, u32[]{:S(2)}, u32[]{:S(2)}) collective-permute-start(bf16[2,768,128]{2,1,0:T(8,128)(2,1)S(1)} %collective-permute-done.7.refs_1_), channel_id=1, source_target_pairs={{0,2},{1,7},{2,4},{3,1},{4,6},{5,3},{6,0},{7,5},{8,10},{9,15},{10,... | collective-permute-start | bytes 1179656 | tf_op jit(solution)/shard_map/ppermute | solution.py:24
  81.1 12.2 %collective-permute-start.3 = (bf16[2,768,128]{2,1,0:T(8,128)(2,1)S(1)}, bf16[2,768,128]{2,1,0:T(8,128)(2,1)S(1)}, u32[]{:S(2)}, u32[]{:S(2)}) collective-permute-start(bf16[2,768,128]{2,1,0:T(8,128)(2,1)S(1)} %collective-permute-done.2.refs_2_), channel_id=1, source_target_pairs={{0,2},{1,7},{2,4},{3,1},{4,6},{5,3},{6,0},{7,5},{8,10},{9,15},{10,... | collective-permute-start | bytes 1179656 | tf_op jit(solution)/shard_map/ppermute | solution.py:24
  86.1 13.6 %collective-permute-start.9 = (bf16[2,768,128]{2,1,0:T(8,128)(2,1)S(1)}, bf16[2,768,128]{2,1,0:T(8,128)(2,1)S(1)}, u32[]{:S(2)}, u32[]{:S(2)}) collective-permute-start(bf16[2,768,128]{2,1,0:T(8,128)(2,1)S(1)} %collective-permute-done.8.refs_2_), channel_id=1, source_target_pairs={{0,2},{1,7},{2,4},{3,1},{4,6},{5,3},{6,0},{7,5},{8,10},{9,15},{10,... | collective-permute-start | bytes 1179656 | tf_op jit(solution)/shard_map/ppermute | solution.py:24
  91.1 8.7 %copy-start.6 = (bf16[2,256,768]{2,1,0:T(8,128)(2,1)}, bf16[2,256,768]{2,1,0:T(8,128)(2,1)S(1)}, u32[]{:S(2)}) copy-start(bf16[2,256,768]{2,1,0:T(8,128)(2,1)S(1)} %collective-permute-done.12.refs_1_) | copy-start | bytes 2359300
  91.1 13.1 %collective-permute-start.13 = (bf16[2,256,768]{2,1,0:T(8,128)(2,1)S(1)}, bf16[2,256,768]{2,1,0:T(8,128)(2,1)}, u32[]{:S(2)}, u32[]{:S(2)}) collective-permute-start(bf16[2,256,768]{2,1,0:T(8,128)(2,1)S(1)} %collective-permute-done.12.refs_1_), channel_id=1, source_target_pairs={{0,128},{1,385},{128,256},{129,1},{256,384},{257,129},{384,0},{385... | collective-permute-start | bytes 2359304 | tf_op jit(solution)/shard_map/ppermute | solution.py:24
  93.4 10.8 %copy-start.8 = (bf16[2,256,768]{2,1,0:T(8,128)(2,1)}, bf16[2,256,768]{2,1,0:T(8,128)(2,1)S(1)}, u32[]{:S(2)}) copy-start(bf16[2,256,768]{2,1,0:T(8,128)(2,1)S(1)} %collective-permute-done.17.refs_1_) | copy-start | bytes 2359300
  93.5 19.2 %collective-permute-start.18 = (bf16[2,256,768]{2,1,0:T(8,128)(2,1)S(1)}, bf16[2,256,768]{2,1,0:T(8,128)(2,1)}, u32[]{:S(2)}, u32[]{:S(2)}) collective-permute-start(bf16[2,256,768]{2,1,0:T(8,128)(2,1)S(1)} %collective-permute-done.17.refs_1_), channel_id=1, source_target_pairs={{0,128},{1,385},{128,256},{129,1},{256,384},{257,129},{384,0},{385... | collective-permute-start | bytes 2359304 | tf_op jit(solution)/shard_map/ppermute | solution.py:24
  95.6 35.5 %collective-permute-start.4 = (bf16[8,768,128]{2,1,0:T(8,128)(2,1)S(1)}, bf16[8,768,128]{2,1,0:T(8,128)(2,1)}, u32[]{:S(2)}, u32[]{:S(2)}) collective-permute-start(bf16[8,768,128]{2,1,0:T(8,128)(2,1)S(1)} %shard_map.75.refs_0_), channel_id=1, source_target_pairs={{0,1},{1,0},{2,3},{3,2},{4,5},{5,4},{6,7},{7,6},{8,9},{9,8},{10,11... | collective-permute-start | bytes 4718600 | tf_op jit(solution)/shard_map/ppermute | solution.py:28
  99.8 31.3 %collective-permute-start.10 = (bf16[8,768,128]{2,1,0:T(8,128)(2,1)S(1)}, bf16[8,768,128]{2,1,0:T(8,128)(2,1)}, u32[]{:S(2)}, u32[]{:S(2)}) collective-permute-start(bf16[8,768,128]{2,1,0:T(8,128)(2,1)S(1)} %shard_map.77.refs_2_), channel_id=1, source_target_pairs={{0,1},{1,0},{2,3},{3,2},{4,5},{5,4},{6,7},{7,6},{8,9},{9,8},{10,11... | collective-permute-start | bytes 4718600 | tf_op jit(solution)/shard_map/ppermute | solution.py:28
  104.3 16.9 %collective-permute-start.14 = (bf16[2,256,768]{2,1,0:T(8,128)(2,1)}, bf16[2,256,768]{2,1,0:T(8,128)(2,1)}, u32[]{:S(2)}, u32[]{:S(2)}) collective-permute-start(bf16[2,256,768]{2,1,0:T(8,128)(2,1)} %collective-permute-done.13.refs_2_), channel_id=1, source_target_pairs={{0,128},{1,385},{128,256},{129,1},{256,384},{257,129},{384,0},{385... | collective-permute-start | bytes 2359304 | tf_op jit(solution)/shard_map/ppermute | solution.py:24
  112.7 16.9 %collective-permute-start.19 = (bf16[2,256,768]{2,1,0:T(8,128)(2,1)}, bf16[2,256,768]{2,1,0:T(8,128)(2,1)}, u32[]{:S(2)}, u32[]{:S(2)}) collective-permute-start(bf16[2,256,768]{2,1,0:T(8,128)(2,1)} %collective-permute-done.18.refs_2_), channel_id=1, source_target_pairs={{0,128},{1,385},{128,256},{129,1},{256,384},{257,129},{384,0},{385... | collective-permute-start | bytes 2359304 | tf_op jit(solution)/shard_map/ppermute | solution.py:24
  121.1 1.1 copy-start.1
  122.3 1.1 copy-start.7
  123.4 6.2 %copy-start.3 = (bf16[2,256,768]{2,1,0:T(8,128)(2,1)S(1)}, bf16[2,256,768]{2,1,0:T(8,128)(2,1)}, u32[]{:S(2)}) copy-start(bf16[2,256,768]{2,1,0:T(8,128)(2,1)} %copy-done.2) | copy-start | bytes 2359300
  123.4 6.2 %copy-start.9 = (bf16[2,256,768]{2,1,0:T(8,128)(2,1)S(1)}, bf16[2,256,768]{2,1,0:T(8,128)(2,1)}, u32[]{:S(2)}) copy-start(bf16[2,256,768]{2,1,0:T(8,128)(2,1)} %copy-done.8) | copy-start | bytes 2359300
  125.1 6.1 %copy-start.12 = (s32[6,6]{1,0:T(8,128)S(1)}, s32[6,6]{1,0:T(8,128)}, u32[]{:S(2)}) copy-start(s32[6,6]{1,0:T(8,128)} %keep_ref.1) | copy-start | bytes 436
  139.2 1.4 copy-start.4
  172.7 1.7 copy-start.5
